TPU v7x, 128 devices: a whole 4x4x4 slice. The times are simulated.
128 devices in a mesh: tm: 4 (over z), tile: 32 (over x, y, core).
Axes of the slice: x: 4, y: 4, z: 4, core: 2. Of those that a mesh axis runs over, the one named last changes fastest.
Arguments:
- multiplier: float32 [4, 4, 1536, 1536], P('tm', None, 'tile'), may hold values from -7 to 7
- obs_dual: float32 [4, 4096], P('tm', 'tile'), may hold values from -6 to 6
- increment: float32 [4, 4, 1536, 1536], P('tm', None, 'tile'), may hold values from -6 to 6
- error_var: float32 [4, 4, 1536, 1536], P('tm', None, 'tile'), may hold values from 0.3 to 3
- obs_var: float32 [4, 4096], P('tm', 'tile'), may hold values from 0.1 to 1
- winds: bfloat16 [4, 2, 4, 1536, 1536], P('tm', None, None, 'tile'), may hold values from -0.29882812 to 0.29882812
- wake_mask: int32 [1536, 1536], P('tile'), may hold values 0 or 1
- obs_cell: int32 [4, 4096], P('tm', 'tile'), may hold values from 0 to 294911
Outputs:
- out_multiplier: float32 [4, 4, 1536, 1536], P('tm', None, 'tile')
- out_obs: float32 [4, 4096], P('tm', 'tile')
- out_increment: float32 [4, 4, 1536, 1536], P('tm', None, 'tile')
- curvature: float32 [], replicated
Inputs may be any that keep to these rules, and one draw needn't show every extreme that they name: `obs_cell`: entries of block j // 128 name a cell of strip j // 128, as (level 48 + row) * 1536 + column with the row counted within the strip; several observations may share a cell.
All inputs are finite; a program needn't handle non-finite values. No bound on the sum of `wake_mask` on one device may be relied on, other than what follows from the above.
Results may differ from a plain program's by a relative error of at most 0.0003.
Values sent between devices are 32-bit elements; how exact they have to be, the bound alone decides.
No kernel may reach another device: no remote copies, remote signals or barrier semaphores. Data moves between devices by JAX's collectives and lax.ppermute only.
A program may use at most 128 MiB of HBM per device.

v0:
```python
import jax
import jax.numpy as jnp
from jax import lax
from jax.sharding import PartitionSpec as P

SUB = 6


kappa_base = 0.04
vertical_mix = 0.05


def padded_2(cells, sides, width):
    for axis, dim in sides:
        count = lax.axis_size(axis)
        ends = count - 1
        head = lax.slice_in_dim(cells, 0, width, axis=dim)
        tail = lax.slice_in_dim(cells, cells.shape[dim] - width, cells.shape[dim], axis=dim)
        cells = jnp.concatenate(
            [
                lax.ppermute(tail, axis, [(i, (i + 1) % count) for i in range(ends)]),
                cells,
                lax.ppermute(head, axis, [((i + 1) % count, i) for i in range(ends)]),
            ],
            axis=dim,
        )
    return cells


def from_behind(value, axis, steps):
    count = lax.axis_size(axis)
    first, last = (max(0, -steps), min(count, count - steps))
    return lax.ppermute(value, axis, [(source, source + steps) for source in range(first, last)])


def coefficients(wind, wake):
    speed_x = wind[0].astype(jnp.float32)
    speed_y = wind[1].astype(jnp.float32)
    diffusion = jnp.broadcast_to(kappa_base * (1.0 + 2.0 * wake.astype(jnp.float32)), speed_x.shape)
    return jnp.stack(
        [
            jnp.maximum(speed_x, 0.0),
            jnp.minimum(speed_x, 0.0),
            jnp.maximum(speed_y, 0.0),
            jnp.minimum(speed_y, 0.0),
            diffusion,
        ]
    )


def substep(padded, coeffs):
    middle = padded[:, 1:-1]
    prior = padded[:, :-2]
    later = padded[:, 2:]
    sideways = jnp.pad(middle, ((0, 0), (0, 0), (1, 1)))
    leftward = sideways[:, :, :-2]
    rightward = sideways[:, :, 2:]
    vertical = jnp.pad(middle, ((1, 1), (0, 0), (0, 0)))
    beneath = vertical[:-2]
    overhead = vertical[2:]
    return (
        middle
        - coeffs[0] * (middle - prior)
        - coeffs[1] * (later - middle)
        - coeffs[2] * (middle - leftward)
        - coeffs[3] * (rightward - middle)
        + coeffs[4] * (prior + later + leftward + rightward - 4.0 * middle)
        + vertical_mix * (beneath + overhead - 2.0 * middle)
    )


def each_model(field, coeffs):
    for section in range(SUB):
        padded = padded_2(field, (("tile", 1),), 1)
        field = substep(padded, coeffs)
    return field


def adjoint_model(field, coeffs):
    levels, rows, columns = field.shape
    for section in range(SUB):
        anchor = jnp.zeros((levels, rows + 2, columns), jnp.float32)
        _, pull = jax.vjp(lambda padded: substep(padded, coeffs), anchor)
        cotangent = pull(field)[0]
        rims = jnp.stack([cotangent[:, 0], cotangent[:, -1]], axis=1)
        beside_all = padded_2(rims, (("tile", 1),), 1)
        field = cotangent[:, 1:-1]
        field = field.at[:, 0].add(beside_all[:, 0])
        field = field.at[:, -1].add(beside_all[:, 3])
    return field


def shards(multiplier, obs_dual, increment, error_var, obs_var, winds, wake_mask, obs_cell):
    coeffs = coefficients(winds[0], wake_mask)
    field = increment[0]
    incoming = from_behind(multiplier[0], "tm", -1)
    moved = each_model(field, coeffs)
    backward = adjoint_model(incoming, coeffs)
    shifted = from_behind(moved, "tm", 1)
    linear_part = field - shifted
    out_mult = error_var[0] * multiplier[0] + linear_part
    flat = field.reshape(-1)
    sampled = flat[obs_cell[0]]
    out_obs = obs_var[0] * obs_dual[0] + sampled
    spread = (
        jnp.zeros(flat.shape, jnp.float32).at[obs_cell[0]].add(obs_dual[0]).reshape(field.shape)
    )
    out_inc = multiplier[0] - backward + spread
    count = lax.axis_size("tm") * lax.axis_size("tile") * (2 * field.size + obs_dual.shape[1])
    local_sum = (
        jnp.sum(multiplier[0] * out_mult)
        + jnp.sum(obs_dual[0] * out_obs)
        + jnp.sum(field * out_inc)
    )
    total = lax.psum(local_sum, ("tm", "tile"))
    curvature = total / jnp.float32(count)
    return (out_mult[None], out_obs[None], out_inc[None], curvature)


def solution(mesh):
    return jax.shard_map(
        shards,
        mesh=mesh,
        in_specs=(
            P("tm", None, "tile", None),
            P("tm", "tile"),
            P("tm", None, "tile", None),
            P("tm", None, "tile", None),
            P("tm", "tile"),
            P("tm", None, None, "tile", None),
            P("tile", None),
            P("tm", "tile"),
        ),
        out_specs=(P("tm", None, "tile", None), P("tm", "tile"), P("tm", None, "tile", None), P()),
        check_vma=False,
    )
```

profile of v0, /device:TPU:1, one launch (start us, length us, event | category | flops | bytes accessed | tf_op | source)
XLA Modules:
  0.0 277.6 jit_solution(1809328347472738896)
XLA Ops:
  3.0 4.6 %collective-permute-start = (f32[4,1,1536]{2,1,0:T(1,128)S(1)}, f32[4,1,1536]{2,1,0:T(1,128)S(1)}, u32[]{:S(2)}, u32[]{:S(2)}) collective-permute-start(f32[4,1,1536]{2,1,0:T(1,128)S(1)} %get-tuple-element.208), channel_id=1, source_target_pairs={{0,1},{1,2},{2,3},{3,4},{4,5},{5,6},{6,7},{7,8},{8,9},{9,10},{10,1... | collective-permute-start | bytes 73736 | tf_op jit(solution)/shard_map/ppermute | solution.py:21
  10.5 20.3 %collective-permute-done.13 = f32[4,48,1536]{2,1,0:T(8,128)S(1)} collective-permute-done((f32[4,48,1536]{2,1,0:T(8,128)}, f32[4,48,1536]{2,1,0:T(8,128)S(1)}, u32[]{:S(2)}, u32[]{:S(2)}) %collective-permute-start.13) | collective-permute-done | bytes 1179680 | tf_op jit(solution)/shard_map/ppermute | solution.py:33
  34.3 4.3 %collective-permute-start.14 = (f32[4,1,1536]{2,1,0:T(1,128)S(1)}, f32[4,1,1536]{2,1,0:T(1,128)S(1)}, u32[]{:S(2)}, u32[]{:S(2)}) collective-permute-start(f32[4,1,1536]{2,1,0:T(1,128)S(1)} %get-tuple-element.163), channel_id=1, source_target_pairs={{0,1},{1,2},{2,3},{3,4},{4,5},{5,6},{6,7},{7,8},{8,9},{9,10},{10,1... | collective-permute-start | bytes 73736 | tf_op jit(solution)/shard_map/ppermute | solution.py:21
  41.3 2.9 %collective-permute-done.15 = f32[4,1,1536]{2,1,0:T(1,128)S(1)} collective-permute-done((f32[4,1,1536]{2,1,0:T(1,128)S(1)}, f32[4,1,1536]{2,1,0:T(1,128)S(1)}, u32[]{:S(2)}, u32[]{:S(2)}) %collective-permute-start.15) | collective-permute-done | bytes 24608 | tf_op jit(solution)/shard_map/ppermute | solution.py:23
  49.1 2.4 collective-permute-start.17
  51.8 2.4 collective-permute-done.17
  59.0 2.4 collective-permute-start.19
  61.7 2.4 collective-permute-done.19
  70.0 2.7 collective-permute-start.21
  79.2 3.3 %fusion.164 = (f32[4,48,1536]{2,1,0:T(8,128)S(1)}, f32[4,48,1536]{2,1,0:T(8,128)S(1)}, f32[4,48,1536]{2,1,0:T(8,128)S(1)}, f32[4,48,1536]{2,1,0:T(8,128)S(1)}, f...) fusion(f32[4,48,1536]{2,1,0:T(8,128)} %scatter-add.59, f32[48,1536]{1,0:T(8,128)S(1)} %add_multiply_fusion, ...), kind=kLoop, calls=%fused_computation.240 | loop fusion | flops 13271040 | bytes 10960896 | tf_op jit(solution)/shard_map/transpose(jvp())/add_any | solution.py:64
  84.1 2.4 collective-permute-start.22
  88.6 5.3 %collective-permute-start.2 = (f32[4,1,1536]{2,1,0:T(1,128)S(1)}, f32[4,1,1536]{2,1,0:T(1,128)S(1)}, u32[]{:S(2)}, u32[]{:S(2)}) collective-permute-start(f32[4,1,1536]{2,1,0:T(1,128)S(1)} %get-tuple-element.206), channel_id=1, source_target_pairs={{0,1},{1,2},{2,3},{3,4},{4,5},{5,6},{6,7},{7,8},{8,9},{9,10},{10,1... | collective-permute-start | bytes 73736 | tf_op jit(solution)/shard_map/ppermute | solution.py:21
  96.4 2.6 collective-permute-done.3
  99.1 6.7 %fusion.162 = (f32[4,48,1536]{2,1,0:T(8,128)}, f32[4,48,1536]{2,1,0:T(8,128)S(1)}, f32[4,48,1536]{2,1,0:T(8,128)S(1)}, f32[4,48,1536]{2,1,0:T(8,128)}, f32[4,48,...) fusion(f32[4,48,1536]{2,1,0:T(8,128)S(1)} %scatter-add.61, f32[48,1536]{1,0:T(8,128)S(1)} %add_multiply_fusion, ...), kind=kLoop, calls=%fused_computation.238 | loop fusion | flops 13271040 | bytes 10960896 | tf_op jit(solution)/shard_map/transpose(jvp())/add_any | solution.py:64
  105.8 3.2 %collective-permute-start.4 = (f32[4,1,1536]{2,1,0:T(1,128)S(1)}, f32[4,1,1536]{2,1,0:T(1,128)S(1)}, u32[]{:S(2)}, u32[]{:S(2)}) collective-permute-start(f32[4,1,1536]{2,1,0:T(1,128)S(1)} %get-tuple-element.204), channel_id=1, source_target_pairs={{0,1},{1,2},{2,3},{3,4},{4,5},{5,6},{6,7},{7,8},{8,9},{9,10},{10,1... | collective-permute-start | bytes 73736 | tf_op jit(solution)/shard_map/ppermute | solution.py:21
  110.9 4.0 %collective-permute-done.5 = f32[4,1,1536]{2,1,0:T(1,128)S(1)} collective-permute-done((f32[4,1,1536]{2,1,0:T(1,128)S(1)}, f32[4,1,1536]{2,1,0:T(1,128)S(1)}, u32[]{:S(2)}, u32[]{:S(2)}) %collective-permute-start.5) | collective-permute-done | bytes 24608 | tf_op jit(solution)/shard_map/ppermute | solution.py:23
  115.0 3.8 %fusion.106 = (f32[4,48,1536]{2,1,0:T(8,128)S(1)}, f32[4,48,1536]{2,1,0:T(8,128)S(1)}) fusion(f32[4,48,1536]{2,1,0:T(8,128)S(1)} %get-tuple-element.166, f32[4,48,1536]{2,1,0:T(8,128)S(1)} %get-tuple-element.165, f32[4,48,1536]{2,1,0:T(8,128)S(1)} %get-tuple-element.192, f32[4,48,1536]{2,1,0:T(8,128)} %copy-done.5, f32[48,1536]{1,0:T(8,128)S(1)} %add_multiply_fusion, ...), kind=kLoop, calls=%fused_computation.143 | loop fusion | flops 15925248 | bytes 9781248 | tf_op jit(solution)/shard_map/transpose(jvp())/add_any | solution.py:55
  118.8 2.4 collective-permute-start.6
  123.2 4.8 %collective-permute-done.7 = f32[4,1,1536]{2,1,0:T(1,128)S(1)} collective-permute-done((f32[4,1,1536]{2,1,0:T(1,128)S(1)}, f32[4,1,1536]{2,1,0:T(1,128)S(1)}, u32[]{:S(2)}, u32[]{:S(2)}) %collective-permute-start.7) | collective-permute-done | bytes 24608 | tf_op jit(solution)/shard_map/ppermute | solution.py:23
  132.7 2.3 collective-permute-start.9
  135.1 2.3 reshape_squeeze.3
  139.5 2.9 %collective-permute-done.9 = f32[4,1,1536]{2,1,0:T(1,128)S(1)} collective-permute-done((f32[4,1,1536]{2,1,0:T(1,128)S(1)}, f32[4,1,1536]{2,1,0:T(1,128)S(1)}, u32[]{:S(2)}, u32[]{:S(2)}) %collective-permute-start.9) | collective-permute-done | bytes 24608 | tf_op jit(solution)/shard_map/ppermute | solution.py:23
  142.5 5.3 %fusion.42 = f32[4,48,1536]{2,1,0:T(8,128)S(1)} fusion(f32[4,48,1536]{2,1,0:T(8,128)} %copy-done.9, f32[4,1,1536]{2,1,0:T(1,128)S(1)} %collective-permute-done.9, f32[4,1,1536]{2,1,0:T(1,128)S(1)} %collective-permute-done.8, f32[48,1536]{1,0:T(8,128)S(1)} %add_multiply_fusion, bf16[1,2,4,48,1536]{4,3,2,1,0:T(8,128)(2,1)S(1)} %copy-done), kind=kLoop, calls=%fused_computation.78 | loop fusion | flops 9437184 | bytes 3883008 | tf_op jit(solution)/shard_map/add | solution.py:62
  148.8 4.9 %collective-permute-start.10 = (f32[4,1,1536]{2,1,0:T(1,128)S(1)}, f32[4,1,1536]{2,1,0:T(1,128)S(1)}, u32[]{:S(2)}, u32[]{:S(2)}) collective-permute-start(f32[4,1,1536]{2,1,0:T(1,128)S(1)} %get-tuple-element.198), channel_id=1, source_target_pairs={{0,1},{1,2},{2,3},{3,4},{4,5},{5,6},{6,7},{7,8},{8,9},{9,10},{10,1... | collective-permute-start | bytes 73736 | tf_op jit(solution)/shard_map/ppermute | solution.py:21
  156.3 2.3 scatter_custom_fusion
  158.6 2.4 reshape.382
  161.0 6.0 %fusion.48 = f32[4,48,1536]{2,1,0:T(8,128)} fusion(f32[4,48,1536]{2,1,0:T(8,128)} %copy-done.8, f32[4,1,1536]{2,1,0:T(1,128)S(1)} %collective-permute-done.11, f32[4,1,1536]{2,1,0:T(1,128)S(1)} %collective-permute-done.10, f32[48,1536]{1,0:T(8,128)S(1)} %add_multiply_fusion, bf16[1,2,4,48,1536]{4,3,2,1,0:T(8,128)(2,1)S(1)} %copy-done), kind=kLoop, calls=%fused_computation.84 | loop fusion | flops 9437184 | bytes 3883008 | tf_op jit(solution)/shard_map/add | solution.py:62
  167.0 4.5 %collective-permute-start.12 = (f32[4,48,1536]{2,1,0:T(8,128)}, f32[4,48,1536]{2,1,0:T(8,128)}, u32[]{:S(2)}, u32[]{:S(2)}) collective-permute-start(f32[4,48,1536]{2,1,0:T(8,128)} %fusion.48), channel_id=1, source_target_pairs={{0,32},{32,64},{64,96},{1,33},{33,65},{65,97},{2,34},{34,66},{66,9... | collective-permute-start | bytes 3538952 | tf_op jit(solution)/shard_map/ppermute | solution.py:33
  171.6 3.9 %collective-permute-start.24 = (f32[4,1,1536]{2,1,0:T(1,128)S(1)}, f32[4,1,1536]{2,1,0:T(1,128)S(1)}, u32[]{:S(2)}, u32[]{:S(2)}) collective-permute-start(f32[4,1,1536]{2,1,0:T(1,128)S(1)} %get-tuple-element.153), channel_id=1, source_target_pairs={{0,1},{1,2},{2,3},{3,4},{4,5},{5,6},{6,7},{7,8},{8,9},{9,10},{10,1... | collective-permute-start | bytes 73736 | tf_op jit(solution)/shard_map/ppermute | solution.py:21
  185.1 8.9 %collective-permute-done.12 = f32[4,48,1536]{2,1,0:T(8,128)} collective-permute-done((f32[4,48,1536]{2,1,0:T(8,128)}, f32[4,48,1536]{2,1,0:T(8,128)}, u32[]{:S(2)}, u32[]{:S(2)}) %collective-permute-start.12) | collective-permute-done | bytes 1179680 | tf_op jit(solution)/shard_map/ppermute | solution.py:33
  194.0 5.3 %multiply_reduce_fusion = (f32[]{:T(128)}, f32[]{:T(128)}, f32[1,4,48,1536]{3,2,1,0:T(8,128)}, f32[1,4,48,1536]{3,2,1,0:T(8,128)}) fusion(f32[1,4,48,1536]{3,2,1,0:T(8,128)S(1)} %copy-done.4, f32[4,48,1536]{2,1,0:T(8,128)} %reshape.382, f32[4,48,1536]{2,1,0:T(8,128)} %scatter-add.78, f32[1,4,48,1536]{3,2,1,0:T(8,128)} %param.32, ...), kind=kLoop, calls=%fused_computation.222 | loop fusion | flops 2654206 | bytes 9437192 | tf_op jit(solution)/shard_map/reduce_sum | solution.py:113
  201.7 74.1 %psum.7 = f32[]{:T(128)} all-reduce(f32[]{:T(128)S(6)} %add.395), channel_id=1, replica_groups=mesh['tm'=4,'tile'=32] {'tm','tile'}, use_global_device_ids=true, to_apply=%region_4.5 | all-reduce | flops 1 | bytes 8 | tf_op jit(solution)/shard_map/psum | solution.py:115
  (120 shorter events, 64.2 us)
Async XLA Ops:
  0.6 30.3 %collective-permute-start.13 = (f32[4,48,1536]{2,1,0:T(8,128)}, f32[4,48,1536]{2,1,0:T(8,128)S(1)}, u32[]{:S(2)}, u32[]{:S(2)}) collective-permute-start(f32[4,48,1536]{2,1,0:T(8,128)} %bitcast.359), channel_id=1, source_target_pairs={{32,0},{64,32},{96,64},{33,1},{65,33},{97,65},{34,2},{66,34},{98,6... | collective-permute-start | bytes 3538952 | tf_op jit(solution)/shard_map/ppermute | solution.py:33
  3.0 76.1 %collective-permute-start = (f32[4,1,1536]{2,1,0:T(1,128)S(1)}, f32[4,1,1536]{2,1,0:T(1,128)S(1)}, u32[]{:S(2)}, u32[]{:S(2)}) collective-permute-start(f32[4,1,1536]{2,1,0:T(1,128)S(1)} %get-tuple-element.208), channel_id=1, source_target_pairs={{0,1},{1,2},{2,3},{3,4},{4,5},{5,6},{6,7},{7,8},{8,9},{9,10},{10,1... | collective-permute-start | bytes 73736 | tf_op jit(solution)/shard_map/ppermute | solution.py:21
  7.6 71.5 %collective-permute-start.1 = (f32[4,1,1536]{2,1,0:T(1,128)S(1)}, f32[4,1,1536]{2,1,0:T(1,128)S(1)}, u32[]{:S(2)}, u32[]{:S(2)}) collective-permute-start(f32[4,1,1536]{2,1,0:T(1,128)S(1)} %get-tuple-element.209), channel_id=1, source_target_pairs={{1,0},{2,1},{3,2},{4,3},{5,4},{6,5},{7,6},{8,7},{9,8},{10,9},{11,1... | collective-permute-start | bytes 73736 | tf_op jit(solution)/shard_map/ppermute | solution.py:23
  10.5 22.5 %copy-start = (bf16[1,2,4,48,1536]{4,3,2,1,0:T(8,128)(2,1)S(1)}, bf16[1,2,4,48,1536]{4,3,2,1,0:T(8,128)(2,1)}, u32[]{:S(2)}) copy-start(bf16[1,2,4,48,1536]{4,3,2,1,0:T(8,128)(2,1)} %param.37) | copy-start | bytes 3538948
  34.3 6.8 %collective-permute-start.14 = (f32[4,1,1536]{2,1,0:T(1,128)S(1)}, f32[4,1,1536]{2,1,0:T(1,128)S(1)}, u32[]{:S(2)}, u32[]{:S(2)}) collective-permute-start(f32[4,1,1536]{2,1,0:T(1,128)S(1)} %get-tuple-element.163), channel_id=1, source_target_pairs={{0,1},{1,2},{2,3},{3,4},{4,5},{5,6},{6,7},{7,8},{8,9},{9,10},{10,1... | collective-permute-start | bytes 73736 | tf_op jit(solution)/shard_map/ppermute | solution.py:21
  39.1 5.1 %collective-permute-start.15 = (f32[4,1,1536]{2,1,0:T(1,128)S(1)}, f32[4,1,1536]{2,1,0:T(1,128)S(1)}, u32[]{:S(2)}, u32[]{:S(2)}) collective-permute-start(f32[4,1,1536]{2,1,0:T(1,128)S(1)} %get-tuple-element.162), channel_id=1, source_target_pairs={{1,0},{2,1},{3,2},{4,3},{5,4},{6,5},{7,6},{8,7},{9,8},{10,9},{11,1... | collective-permute-start | bytes 73736 | tf_op jit(solution)/shard_map/ppermute | solution.py:23
  46.6 4.8 %collective-permute-start.16 = (f32[4,1,1536]{2,1,0:T(1,128)S(1)}, f32[4,1,1536]{2,1,0:T(1,128)S(1)}, u32[]{:S(2)}, u32[]{:S(2)}) collective-permute-start(f32[4,1,1536]{2,1,0:T(1,128)S(1)} %get-tuple-element.161), channel_id=1, source_target_pairs={{0,1},{1,2},{2,3},{3,4},{4,5},{5,6},{6,7},{7,8},{8,9},{9,10},{10,1... | collective-permute-start | bytes 73736 | tf_op jit(solution)/shard_map/ppermute | solution.py:21
  49.1 5.1 %collective-permute-start.17 = (f32[4,1,1536]{2,1,0:T(1,128)S(1)}, f32[4,1,1536]{2,1,0:T(1,128)S(1)}, u32[]{:S(2)}, u32[]{:S(2)}) collective-permute-start(f32[4,1,1536]{2,1,0:T(1,128)S(1)} %get-tuple-element.160), channel_id=1, source_target_pairs={{1,0},{2,1},{3,2},{4,3},{5,4},{6,5},{7,6},{8,7},{9,8},{10,9},{11,1... | collective-permute-start | bytes 73736 | tf_op jit(solution)/shard_map/ppermute | solution.py:23
  56.6 4.8 %collective-permute-start.18 = (f32[4,1,1536]{2,1,0:T(1,128)S(1)}, f32[4,1,1536]{2,1,0:T(1,128)S(1)}, u32[]{:S(2)}, u32[]{:S(2)}) collective-permute-start(f32[4,1,1536]{2,1,0:T(1,128)S(1)} %get-tuple-element.159), channel_id=1, source_target_pairs={{0,1},{1,2},{2,3},{3,4},{4,5},{5,6},{6,7},{7,8},{8,9},{9,10},{10,1... | collective-permute-start | bytes 73736 | tf_op jit(solution)/shard_map/ppermute | solution.py:21
  59.0 5.1 %collective-permute-start.19 = (f32[4,1,1536]{2,1,0:T(1,128)S(1)}, f32[4,1,1536]{2,1,0:T(1,128)S(1)}, u32[]{:S(2)}, u32[]{:S(2)}) collective-permute-start(f32[4,1,1536]{2,1,0:T(1,128)S(1)} %get-tuple-element.158), channel_id=1, source_target_pairs={{1,0},{2,1},{3,2},{4,3},{5,4},{6,5},{7,6},{8,7},{9,8},{10,9},{11,1... | collective-permute-start | bytes 73736 | tf_op jit(solution)/shard_map/ppermute | solution.py:23
  66.6 6.1 %collective-permute-start.20 = (f32[4,1,1536]{2,1,0:T(1,128)S(1)}, f32[4,1,1536]{2,1,0:T(1,128)S(1)}, u32[]{:S(2)}, u32[]{:S(2)}) collective-permute-start(f32[4,1,1536]{2,1,0:T(1,128)S(1)} %get-tuple-element.157), channel_id=1, source_target_pairs={{0,1},{1,2},{2,3},{3,4},{4,5},{5,6},{6,7},{7,8},{8,9},{9,10},{10,1... | collective-permute-start | bytes 73736 | tf_op jit(solution)/shard_map/ppermute | solution.py:21
  70.0 6.5 %collective-permute-start.21 = (f32[4,1,1536]{2,1,0:T(1,128)S(1)}, f32[4,1,1536]{2,1,0:T(1,128)S(1)}, u32[]{:S(2)}, u32[]{:S(2)}) collective-permute-start(f32[4,1,1536]{2,1,0:T(1,128)S(1)} %get-tuple-element.156), channel_id=1, source_target_pairs={{1,0},{2,1},{3,2},{4,3},{5,4},{6,5},{7,6},{8,7},{9,8},{10,9},{11,1... | collective-permute-start | bytes 73736 | tf_op jit(solution)/shard_map/ppermute | solution.py:23
  84.1 11.7 %collective-permute-start.22 = (f32[4,1,1536]{2,1,0:T(1,128)S(1)}, f32[4,1,1536]{2,1,0:T(1,128)S(1)}, u32[]{:S(2)}, u32[]{:S(2)}) collective-permute-start(f32[4,1,1536]{2,1,0:T(1,128)S(1)} %get-tuple-element.155), channel_id=1, source_target_pairs={{0,1},{1,2},{2,3},{3,4},{4,5},{5,6},{6,7},{7,8},{8,9},{9,10},{10,1... | collective-permute-start | bytes 73736 | tf_op jit(solution)/shard_map/ppermute | solution.py:21
  86.6 9.5 %collective-permute-start.23 = (f32[4,1,1536]{2,1,0:T(1,128)S(1)}, f32[4,1,1536]{2,1,0:T(1,128)S(1)}, u32[]{:S(2)}, u32[]{:S(2)}) collective-permute-start(f32[4,1,1536]{2,1,0:T(1,128)S(1)} %get-tuple-element.154), channel_id=1, source_target_pairs={{1,0},{2,1},{3,2},{4,3},{5,4},{6,5},{7,6},{8,7},{9,8},{10,9},{11,1... | collective-permute-start | bytes 73736 | tf_op jit(solution)/shard_map/ppermute | solution.py:23
  88.6 7.8 %collective-permute-start.2 = (f32[4,1,1536]{2,1,0:T(1,128)S(1)}, f32[4,1,1536]{2,1,0:T(1,128)S(1)}, u32[]{:S(2)}, u32[]{:S(2)}) collective-permute-start(f32[4,1,1536]{2,1,0:T(1,128)S(1)} %get-tuple-element.206), channel_id=1, source_target_pairs={{0,1},{1,2},{2,3},{3,4},{4,5},{5,6},{6,7},{7,8},{8,9},{9,10},{10,1... | collective-permute-start | bytes 73736 | tf_op jit(solution)/shard_map/ppermute | solution.py:21
  93.9 5.1 %collective-permute-start.3 = (f32[4,1,1536]{2,1,0:T(1,128)S(1)}, f32[4,1,1536]{2,1,0:T(1,128)S(1)}, u32[]{:S(2)}, u32[]{:S(2)}) collective-permute-start(f32[4,1,1536]{2,1,0:T(1,128)S(1)} %get-tuple-element.207), channel_id=1, source_target_pairs={{1,0},{2,1},{3,2},{4,3},{5,4},{6,5},{7,6},{8,7},{9,8},{10,9},{11,1... | collective-permute-start | bytes 73736 | tf_op jit(solution)/shard_map/ppermute | solution.py:23
  105.8 5.2 %collective-permute-start.4 = (f32[4,1,1536]{2,1,0:T(1,128)S(1)}, f32[4,1,1536]{2,1,0:T(1,128)S(1)}, u32[]{:S(2)}, u32[]{:S(2)}) collective-permute-start(f32[4,1,1536]{2,1,0:T(1,128)S(1)} %get-tuple-element.204), channel_id=1, source_target_pairs={{0,1},{1,2},{2,3},{3,4},{4,5},{5,6},{6,7},{7,8},{8,9},{9,10},{10,1... | collective-permute-start | bytes 73736 | tf_op jit(solution)/shard_map/ppermute | solution.py:21
  109.0 6.0 %collective-permute-start.5 = (f32[4,1,1536]{2,1,0:T(1,128)S(1)}, f32[4,1,1536]{2,1,0:T(1,128)S(1)}, u32[]{:S(2)}, u32[]{:S(2)}) collective-permute-start(f32[4,1,1536]{2,1,0:T(1,128)S(1)} %get-tuple-element.205), channel_id=1, source_target_pairs={{1,0},{2,1},{3,2},{4,3},{5,4},{6,5},{7,6},{8,7},{9,8},{10,9},{11,1... | collective-permute-start | bytes 73736 | tf_op jit(solution)/shard_map/ppermute | solution.py:23
  118.8 4.4 %collective-permute-start.6 = (f32[4,1,1536]{2,1,0:T(1,128)S(1)}, f32[4,1,1536]{2,1,0:T(1,128)S(1)}, u32[]{:S(2)}, u32[]{:S(2)}) collective-permute-start(f32[4,1,1536]{2,1,0:T(1,128)S(1)} %get-tuple-element.202), channel_id=1, source_target_pairs={{0,1},{1,2},{2,3},{3,4},{4,5},{5,6},{6,7},{7,8},{8,9},{9,10},{10,1... | collective-permute-start | bytes 73736 | tf_op jit(solution)/shard_map/ppermute | solution.py:21
  121.2 6.8 %collective-permute-start.7 = (f32[4,1,1536]{2,1,0:T(1,128)S(1)}, f32[4,1,1536]{2,1,0:T(1,128)S(1)}, u32[]{:S(2)}, u32[]{:S(2)}) collective-permute-start(f32[4,1,1536]{2,1,0:T(1,128)S(1)} %get-tuple-element.203), channel_id=1, source_target_pairs={{1,0},{2,1},{3,2},{4,3},{5,4},{6,5},{7,6},{8,7},{9,8},{10,9},{11,1... | collective-permute-start | bytes 73736 | tf_op jit(solution)/shard_map/ppermute | solution.py:23
  130.7 8.8 %collective-permute-start.8 = (f32[4,1,1536]{2,1,0:T(1,128)S(1)}, f32[4,1,1536]{2,1,0:T(1,128)S(1)}, u32[]{:S(2)}, u32[]{:S(2)}) collective-permute-start(f32[4,1,1536]{2,1,0:T(1,128)S(1)} %get-tuple-element.200), channel_id=1, source_target_pairs={{0,1},{1,2},{2,3},{3,4},{4,5},{5,6},{6,7},{7,8},{8,9},{9,10},{10,1... | collective-permute-start | bytes 73736 | tf_op jit(solution)/shard_map/ppermute | solution.py:21
  132.7 9.7 %collective-permute-start.9 = (f32[4,1,1536]{2,1,0:T(1,128)S(1)}, f32[4,1,1536]{2,1,0:T(1,128)S(1)}, u32[]{:S(2)}, u32[]{:S(2)}) collective-permute-start(f32[4,1,1536]{2,1,0:T(1,128)S(1)} %get-tuple-element.201), channel_id=1, source_target_pairs={{1,0},{2,1},{3,2},{4,3},{5,4},{6,5},{7,6},{8,7},{9,8},{10,9},{11,1... | collective-permute-start | bytes 73736 | tf_op jit(solution)/shard_map/ppermute | solution.py:23
  139.5 16.1 %copy-start.10 = (f32[1,128]{1,0:T(1,128)S(1)}, f32[1,128]{1,0:T(1,128)}, u32[]{:S(2)}) copy-start(f32[1,128]{1,0:T(1,128)} %param.33) | copy-start | bytes 1540
  139.5 16.1 %copy-start.11 = (f32[1,128]{1,0:T(1,128)S(1)}, f32[1,128]{1,0:T(1,128)}, u32[]{:S(2)}) copy-start(f32[1,128]{1,0:T(1,128)} %param.36) | copy-start | bytes 1540
  148.8 12.2 %collective-permute-start.10 = (f32[4,1,1536]{2,1,0:T(1,128)S(1)}, f32[4,1,1536]{2,1,0:T(1,128)S(1)}, u32[]{:S(2)}, u32[]{:S(2)}) collective-permute-start(f32[4,1,1536]{2,1,0:T(1,128)S(1)} %get-tuple-element.198), channel_id=1, source_target_pairs={{0,1},{1,2},{2,3},{3,4},{4,5},{5,6},{6,7},{7,8},{8,9},{9,10},{10,1... | collective-permute-start | bytes 73736 | tf_op jit(solution)/shard_map/ppermute | solution.py:21
  153.7 7.3 %collective-permute-start.11 = (f32[4,1,1536]{2,1,0:T(1,128)S(1)}, f32[4,1,1536]{2,1,0:T(1,128)S(1)}, u32[]{:S(2)}, u32[]{:S(2)}) collective-permute-start(f32[4,1,1536]{2,1,0:T(1,128)S(1)} %get-tuple-element.199), channel_id=1, source_target_pairs={{1,0},{2,1},{3,2},{4,3},{5,4},{6,5},{7,6},{8,7},{9,8},{10,9},{11,1... | collective-permute-start | bytes 73736 | tf_op jit(solution)/shard_map/ppermute | solution.py:23
  161.0 10.6 %copy-start.1 = (f32[4,48,1536]{2,1,0:T(8,128)S(1)}, f32[4,48,1536]{2,1,0:T(8,128)}, u32[]{:S(2)}) copy-start(f32[4,48,1536]{2,1,0:T(8,128)} %get-tuple-element.164) | copy-start | bytes 3538948
  161.0 10.6 %copy-start.2 = (f32[4,48,1536]{2,1,0:T(8,128)S(1)}, f32[4,48,1536]{2,1,0:T(8,128)}, u32[]{:S(2)}) copy-start(f32[4,48,1536]{2,1,0:T(8,128)} %get-tuple-element.167) | copy-start | bytes 3538948
  167.0 27.0 %collective-permute-start.12 = (f32[4,48,1536]{2,1,0:T(8,128)}, f32[4,48,1536]{2,1,0:T(8,128)}, u32[]{:S(2)}, u32[]{:S(2)}) collective-permute-start(f32[4,48,1536]{2,1,0:T(8,128)} %fusion.48), channel_id=1, source_target_pairs={{0,32},{32,64},{64,96},{1,33},{33,65},{65,97},{2,34},{34,66},{66,9... | collective-permute-start | bytes 3538952 | tf_op jit(solution)/shard_map/ppermute | solution.py:33
  171.6 7.5 %collective-permute-start.24 = (f32[4,1,1536]{2,1,0:T(1,128)S(1)}, f32[4,1,1536]{2,1,0:T(1,128)S(1)}, u32[]{:S(2)}, u32[]{:S(2)}) collective-permute-start(f32[4,1,1536]{2,1,0:T(1,128)S(1)} %get-tuple-element.153), channel_id=1, source_target_pairs={{0,1},{1,2},{2,3},{3,4},{4,5},{5,6},{6,7},{7,8},{8,9},{9,10},{10,1... | collective-permute-start | bytes 73736 | tf_op jit(solution)/shard_map/ppermute | solution.py:21
  177.0 16.9 %copy-start.4 = (f32[1,4,48,1536]{3,2,1,0:T(8,128)S(1)}, f32[1,4,48,1536]{3,2,1,0:T(8,128)}, u32[]{:S(2)}) copy-start(f32[1,4,48,1536]{3,2,1,0:T(8,128)} %param.34) | copy-start | bytes 3538948
  177.0 5.4 %collective-permute-start.25 = (f32[4,1,1536]{2,1,0:T(1,128)S(1)}, f32[4,1,1536]{2,1,0:T(1,128)S(1)}, u32[]{:S(2)}, u32[]{:S(2)}) collective-permute-start(f32[4,1,1536]{2,1,0:T(1,128)S(1)} %get-tuple-element.152), channel_id=1, source_target_pairs={{1,0},{2,1},{3,2},{4,3},{5,4},{6,5},{7,6},{8,7},{9,8},{10,9},{11,1... | collective-permute-start | bytes 73736 | tf_op jit(solution)/shard_map/ppermute | solution.py:23
  (7 other events, 38.1 us)
where the time goes:
time: 279 us; the launch traced here: 278 us
  blocking collectives  74.1 us (27%)
  starting transfers between devices  70 us (25%)
  waiting for transfers between devices  55.1 us (20%)
  other arithmetic  52 us (19%)
  local copies, waits for them, and re-layouts  21.3 us (8%)
  between operations  5.14 us (2%)
    psum x1, blocking collectives, shards(): total = lax.psum(local_sum, ('tm', 'tile'))  74.1 us
    ppermute x12, starting transfers between devices, padded_2(): lax.ppermute(tail, axis, [(i, (i + 1) % count) for i in range(ends)])  38.8 us
    ppermute x2, waiting for transfers between devices, from_behind(): lax.ppermute(value, axis, [(source, source + steps) for source in range(f...  29.2 us
    ppermute x12, waiting for transfers between devices, padded_2(): lax.ppermute(head, axis, [((i + 1) % count, i) for i in range(ends)])  25.8 us
    ppermute x12, starting transfers between devices, padded_2(): lax.ppermute(head, axis, [((i + 1) % count, i) for i in range(ends)])  25.4 us
    add_any x6, other arithmetic, substep(): later - middle  14.8 us
    add x3, other arithmetic, substep(): middle - coeffs[0] * (middle - prior) - coeffs[1] * (later - middle)  12.9 us
    add_any x6, other arithmetic, substep(): sideways = jnp.pad(middle, ((0, 0), (0, 0), (1, 1)))  9.72 us
  transfers between devices with their start and end apart: 26, of which 11 were waited for; matrix products, arithmetic and copies ran while one was open for 13% of the time, Pallas kernels for 0%

commit v1 on v0

v1 whole, which is shorter than its diff:
```python
import functools

import jax
import jax.numpy as jnp
from jax import lax
from jax.experimental import pallas as pl
from jax.experimental.pallas import tpu as pltpu
from jax.sharding import PartitionSpec as P

SUB = 6
LANES = 128
KAPPA = 0.04
MIX = 0.05
BASE = 16
EDGE = 8
INC, WIND, KD, MULT = 0, 4, 12, 13
CHANNELS = 17
MIB = 2**20


def call(body, out_shape, *args, scratch=(), in_specs=None, vmem=48, flops=1000, grid=None):
    kwargs = {}
    if in_specs is not None:
        kwargs["in_specs"] = in_specs
    if grid is not None:
        kwargs["grid"] = grid
    return pl.pallas_call(
        body,
        out_shape=out_shape,
        scratch_shapes=list(scratch),
        compiler_params=pltpu.CompilerParams(vmem_limit_bytes=vmem * MIB),
        cost_estimate=pl.CostEstimate(flops=flops, bytes_accessed=1000, transcendentals=0),
        **kwargs,
    )(*args)


def f32(*shape):
    return jax.ShapeDtypeStruct(shape, jnp.float32)


def cols(j):
    return pl.ds(j * LANES, LANES)


def diffusion_of(wake):
    return KAPPA * (1.0 + 2.0 * wake.astype(jnp.float32))


def put_coeffs(coef, u, v, kd, level, j, row, rows, adjoint):
    north = jnp.maximum(u, 0.0) + kd
    south = kd - jnp.minimum(u, 0.0)
    west = jnp.maximum(v, 0.0) + kd
    east = kd - jnp.minimum(v, 0.0)
    coef[0, level, j, pl.ds(row, rows), :] = (1.0 - 2.0 * MIX) - ((north + south) + (west + east))
    if adjoint:
        coef[1, level, j, pl.ds(row + 1, rows), :] = south
        coef[2, level, j, pl.ds(row - 1, rows), :] = north
        coef[3, level, j, pl.ds(row, rows), :] = east
        coef[4, level, j, pl.ds(row, rows), :] = west
    else:
        coef[1, level, j, pl.ds(row, rows), :] = north
        coef[2, level, j, pl.ds(row, rows), :] = south
        coef[3, level, j, pl.ds(row, rows), :] = west
        coef[4, level, j, pl.ds(row, rows), :] = east


def own_coeffs(coef, winds, wake, tiles, adjoint):
    levels, columns = winds.shape[1], winds.shape[3] // LANES
    for tile in tiles:
        row = tile * 16
        for j in range(columns):
            kd = diffusion_of(wake[pl.ds(row, 16), cols(j)])
            for level in range(levels):
                u = winds[0, level, pl.ds(row, 16), cols(j)].astype(jnp.float32)
                v = winds[1, level, pl.ds(row, 16), cols(j)].astype(jnp.float32)
                put_coeffs(coef, u, v, kd, level, j, BASE + row, 16, adjoint)


def halo_coeffs(coef, halo, row, levels, columns, adjoint):
    for j in range(columns):
        kd = halo[pl.ds(KD * SUB, SUB), cols(j)]
        for level in range(levels):
            u = halo[pl.ds((WIND + level) * SUB, SUB), cols(j)]
            v = halo[pl.ds((WIND + levels + level) * SUB, SUB), cols(j)]
            put_coeffs(coef, u, v, kd, level, j, row, SUB, adjoint)


def substep_tile(src, dst, coef, row, adjoint):
    levels, columns = src.shape[0], src.shape[1]
    lane = lax.broadcasted_iota(jnp.int32, (8, LANES), 1)
    first, last = lane == 0, lane == LANES - 1
    zero = jnp.zeros((8, LANES), jnp.float32)

    def at(k, level, j):
        return coef[k, level, j, pl.ds(row, 8), :]

    def load(j):
        middle = [src[level, j, pl.ds(row, 8), :] for level in range(levels)]
        if adjoint:
            to_east = [at(3, level, j) * middle[level] for level in range(levels)]
            to_west = [at(4, level, j) * middle[level] for level in range(levels)]
        else:
            to_east = to_west = middle
        return (
            middle,
            [pltpu.roll(x, 1, 1) for x in to_east],
            [pltpu.roll(x, LANES - 1, 1) for x in to_west],
        )

    middle, rolled_e, rolled_w = load(0)
    before = [zero] * levels
    for j in range(columns):
        if j + 1 < columns:
            after, after_e, after_w = load(j + 1)
        else:
            after, after_e, after_w = None, None, [zero] * levels
        for level in range(levels):
            west = jnp.where(first, before[level], rolled_e[level])
            east = jnp.where(last, after_w[level], rolled_w[level])
            if not adjoint:
                west = at(3, level, j) * west
                east = at(4, level, j) * east
            total = at(0, level, j) * middle[level]
            total += at(1, level, j) * src[level, j, pl.ds(row - 1, 8), :]
            total += at(2, level, j) * src[level, j, pl.ds(row + 1, 8), :]
            total += west
            total += east
            if level == 0:
                vertical = middle[1]
            elif level == levels - 1:
                vertical = middle[level - 1]
            else:
                vertical = middle[level - 1] + middle[level + 1]
            dst[level, j, pl.ds(row, 8), :] = total + MIX * vertical
        before = rolled_e
        middle, rolled_e, rolled_w = after, after_e, after_w


def run_model(a, b, coef, spans, adjoint):
    for step in range(SUB):
        src, dst = (a, b) if step % 2 == 0 else (b, a)
        reach = SUB - 1 - step
        for low, high in spans:
            start = BASE + low - reach
            tiles = -(-(high - low + 2 * reach) // 8)

            def tile(i, carry, src=src, dst=dst, start=start):
                substep_tile(src, dst, coef, start + i * 8, adjoint)
                return carry

            lax.fori_loop(0, tiles, tile, 0)


def pack_kernel(inc_t, inc_b, mult_t, mult_b, wind_t, wind_b, wake_t, wake_b, top, bottom):
    levels = inc_t.shape[0]
    for out, inc, mult, wind, wake, at in (
        (top, inc_t, mult_t, wind_t, wake_t, 0),
        (bottom, inc_b, mult_b, wind_b, wake_b, 2),
    ):
        for level in range(levels):
            out[pl.ds((INC + level) * SUB, SUB), :] = inc[level, at : at + SUB, :]
            out[pl.ds((MULT + level) * SUB, SUB), :] = mult[level, at : at + SUB, :]
            for part in range(2):
                rows = wind[part, level].astype(jnp.float32)
                first = 0 if at == 0 else 16 - SUB
                out[pl.ds((WIND + part * levels + level) * SUB, SUB), :] = rows[first : first + SUB]
        out[pl.ds(KD * SUB, SUB), :] = diffusion_of(wake[at : at + SUB, :])
        out[pl.ds(CHANNELS * SUB, 2), :] = jnp.zeros((2, out.shape[1]), jnp.float32)


def pack(inc, mult, winds, wake):
    levels, rows, columns = inc.shape
    field = [
        pl.BlockSpec((levels, 8, columns), lambda i, at=at: (0, at, 0))
        for at in (0, rows // 8 - 1)
    ]
    wind = [
        pl.BlockSpec((2, levels, 16, columns), lambda i, at=at: (0, 0, at, 0))
        for at in (0, rows // 16 - 1)
    ]
    mask = [pl.BlockSpec((8, columns), lambda i, at=at: (at, 0)) for at in (0, rows // 8 - 1)]
    message = f32(CHANNELS * SUB + 2, columns)
    return call(
        pack_kernel,
        [message, message],
        inc, inc, mult, mult, winds, winds, wake, wake,
        in_specs=field + field + wind + mask,
        grid=(1,),
    )


def scratch_of(levels, columns, rows=48):
    shape = (levels, columns // LANES, rows + 2 * BASE, LANES)
    return [pltpu.VMEM(shape, jnp.float32)] * 2 + [pltpu.VMEM((5,) + shape, jnp.float32)]


def centre_kernel(inc, winds, wake, out, a, b, coef, *, low, high):
    levels, rows, columns = inc.shape
    tiles = columns // LANES
    own_coeffs(coef, winds, wake, range(rows // 16), False)
    for level in range(levels):
        for j in range(tiles):
            a[level, j, pl.ds(BASE, rows), :] = inc[level, :, cols(j)]
    run_model(a, b, coef, [(low, high)], False)
    for level in range(levels):
        for j in range(tiles):
            out[level, :, cols(j)] = a[level, j, pl.ds(BASE + low, high - low), :]


def forward_centre(inc, winds, wake):
    levels, rows, columns = inc.shape
    low, high = EDGE, rows - EDGE
    return call(
        functools.partial(centre_kernel, low=low, high=high),
        f32(levels, high - low, columns),
        inc, winds, wake,
        scratch=scratch_of(levels, columns, rows),
    )


def edges_kernel(inc, winds, wake, above, below, out, rims, a, b, coef):
    levels, rows, columns = inc.shape
    tiles = columns // LANES
    own_coeffs(coef, winds, wake, (0, rows // 16 - 1), False)
    halo_coeffs(coef, above, BASE - SUB, levels, tiles, False)
    halo_coeffs(coef, below, BASE + rows, levels, tiles, False)
    for level in range(levels):
        part = pl.ds((INC + level) * SUB, SUB)
        rims[pl.ds(level * SUB, SUB), :] = above[pl.ds((MULT + level) * SUB, SUB), :]
        rims[pl.ds((levels + level) * SUB, SUB), :] = below[pl.ds((MULT + level) * SUB, SUB), :]
        for j in range(tiles):
            a[level, j, pl.ds(BASE, 16), :] = inc[level, :16, cols(j)]
            a[level, j, pl.ds(BASE + rows - 16, 16), :] = inc[level, rows - 16 :, cols(j)]
            a[level, j, pl.ds(BASE - SUB, SUB), :] = above[part, cols(j)]
            a[level, j, pl.ds(BASE + rows, SUB), :] = below[part, cols(j)]
    run_model(a, b, coef, [(0, EDGE), (rows - EDGE, rows)], False)
    for level in range(levels):
        for j in range(tiles):
            out[level, :EDGE, cols(j)] = a[level, j, pl.ds(BASE, EDGE), :]
            out[level, EDGE:, cols(j)] = a[level, j, pl.ds(BASE + rows - EDGE, EDGE), :]


def forward_edges(inc, winds, wake, above, below):
    levels, rows, columns = inc.shape
    return call(
        edges_kernel,
        [f32(levels, 2 * EDGE, columns), f32(2 * levels * SUB, columns)],
        inc, winds, wake, above, below,
        scratch=scratch_of(levels, columns, rows),
    )


def one_hots(cell, rows, columns):
    where = lax.broadcasted_iota(jnp.int32, (rows, LANES), 0) * columns
    offset = cell - where
    in_row = (offset >= 0) & (offset < columns)
    column = jnp.sum(jnp.where(in_row, offset, 0), axis=0, keepdims=True)
    in_column = lax.broadcasted_iota(jnp.int32, (columns, LANES), 0) == column
    return in_row, in_column.astype(jnp.float32)


def observe_kernel(inc, dual, var, cell, out, terms):
    levels, rows, columns = inc.shape
    in_row, in_column = one_hots(cell[...], levels * rows, columns)
    picked = jnp.dot(
        inc[...].reshape(levels * rows, columns),
        in_column,
        precision=lax.Precision.HIGHEST,
        preferred_element_type=jnp.float32,
    )
    sampled = jnp.sum(jnp.where(in_row, picked, 0.0), axis=0, keepdims=True)
    value = var[...] * dual[...] + sampled
    out[...] = value
    terms[...] = dual[...] * (value + sampled)


def observe(inc, dual, var, cell):
    shape = f32(*dual.shape)
    return call(observe_kernel, [shape, shape], inc, dual, var, cell)


def sums_kernel(mult, var, inc, incoming, centre, edges, terms, out):
    levels, rows, columns = inc.shape

    def part(moved, level, rows_at, row, total):
        here = pl.ds(row, 8)
        m, q = mult[level, here, :], inc[level, here, :]
        value = m * (var[level, here, :] * m + 2.0 * q)
        value -= 2.0 * (moved[level, pl.ds(rows_at, 8), :] * incoming[level, here, :])
        return total + value

    total = jnp.zeros((8, columns), jnp.float32)
    for level in range(levels):
        for at in range(0, EDGE, 8):
            total = part(edges, level, at, at, total)
            total = part(edges, level, EDGE + at, rows - EDGE + at, total)
        for at in range(0, rows - 2 * EDGE, 8):
            total = part(centre, level, at, EDGE + at, total)
    out[...] = jnp.full(out.shape, jnp.sum(total) + jnp.sum(terms[...]), jnp.float32)


def sums(count, mult, var, inc, incoming, centre, edges, terms):
    return call(sums_kernel, f32(count, LANES), mult, var, inc, incoming, centre, edges, terms)


def adjoint_kernel(
    incoming, rims, winds, wake, above, below, mult, dual, cell, out, a, b, coef
):
    levels, rows, columns = incoming.shape
    tiles = columns // LANES
    own_coeffs(coef, winds, wake, range(rows // 16), True)
    halo_coeffs(coef, above, BASE - SUB, levels, tiles, True)
    halo_coeffs(coef, below, BASE + rows, levels, tiles, True)
    for level in range(levels):
        for j in range(tiles):
            a[level, j, pl.ds(BASE, rows), :] = incoming[level, :, cols(j)]
            a[level, j, pl.ds(BASE - SUB, SUB), :] = rims[pl.ds(level * SUB, SUB), cols(j)]
            a[level, j, pl.ds(BASE + rows, SUB), :] = rims[
                pl.ds((levels + level) * SUB, SUB), cols(j)
            ]
    run_model(a, b, coef, [(0, rows)], True)
    in_row, in_column = one_hots(cell[...], levels * rows, columns)
    spread = lax.dot_general(
        jnp.where(in_row, dual[...], 0.0),
        in_column,
        (((1,), (1,)), ((), ())),
        precision=lax.Precision.HIGHEST,
        preferred_element_type=jnp.float32,
    )
    out[...] = mult[...] + spread.reshape(out.shape)
    for level in range(levels):
        for j in range(tiles):
            out[level, :, cols(j)] -= a[level, j, pl.ds(BASE, rows), :]


def adjoint(incoming, rims, winds, wake, above, below, mult, dual, cell):
    levels, rows, columns = incoming.shape
    return call(
        adjoint_kernel,
        f32(*incoming.shape),
        incoming, rims, winds, wake, above, below, mult, dual, cell,
        scratch=scratch_of(levels, columns, rows),
    )


def combine_kernel(var, mult, inc, centre, edges, out):
    rows = inc.shape[1]
    middle = pl.ds(EDGE, rows - 2 * EDGE)
    out[:, middle, :] = var[:, middle, :] * mult[:, middle, :] + (inc[:, middle, :] - centre[...])
    for here, there in ((pl.ds(0, EDGE), pl.ds(0, EDGE)), (pl.ds(rows - EDGE, EDGE), pl.ds(EDGE, EDGE))):
        out[:, here, :] = var[:, here, :] * mult[:, here, :] + (inc[:, here, :] - edges[:, there, :])


def combine(var, mult, inc, centre, edges):
    return call(combine_kernel, f32(*inc.shape), var, mult, inc, centre, edges)


def total_kernel(parts, out, *, scale):
    out[0, 0] = jnp.sum(parts[:, 0:1]) * scale


def after(value, *others):
    return lax.optimization_barrier((value, *others))[0]


def shards(multiplier, obs_dual, increment, error_var, obs_var, winds, wake, cell):
    mult, inc, var, wind = multiplier[0], increment[0], error_var[0], winds[0]
    windows, strips = lax.axis_size("tm"), lax.axis_size("tile")
    up = [(k, k + 1) for k in range(windows - 1)]
    down = [(k + 1, k) for k in range(windows - 1)]
    onward = [(t, t + 1) for t in range(strips - 1)]
    backward = [(t + 1, t) for t in range(strips - 1)]

    incoming = lax.ppermute(mult, "tm", down)
    centre = forward_centre(inc, wind, wake)
    centre_in = lax.ppermute(centre, "tm", up)
    top, bottom = pack(after(inc, centre), mult, wind, wake)
    above = lax.ppermute(bottom, "tile", onward)
    below = lax.ppermute(top, "tile", backward)
    out_obs, terms = observe(after(inc, top), obs_dual, obs_var, cell)
    edges, rims = forward_edges(inc, wind, wake, above, below)
    edges_in = lax.ppermute(edges, "tm", up)
    rims_in = lax.ppermute(rims, "tm", down)
    count = windows * strips
    partial = sums(count, mult, var, inc, incoming, centre, edges, terms)
    parts = lax.all_to_all(partial, ("tm", "tile"), 0, 0, tiled=True)
    out_inc = adjoint(incoming, rims_in, wind, wake, above, below, mult, obs_dual, cell)
    out_mult = combine(var, mult, inc, centre_in, edges_in)
    elements = count * (2 * inc.size + obs_dual.shape[1])
    curvature = jnp.sum(parts[:, 0]) / jnp.float32(elements)
    return out_mult[None], out_obs, out_inc[None], curvature


def solution(mesh):
    return jax.shard_map(
        shards,
        mesh=mesh,
        in_specs=(
            P("tm", None, "tile", None),
            P("tm", "tile"),
            P("tm", None, "tile", None),
            P("tm", None, "tile", None),
            P("tm", "tile"),
            P("tm", None, None, "tile", None),
            P("tile", None),
            P("tm", "tile"),
        ),
        out_specs=(P("tm", None, "tile", None), P("tm", "tile"), P("tm", None, "tile", None), P()),
        check_vma=False,
    )
```

time: 279 us -> 78.5 us (0.28)
  blocking collectives: 74.1 us -> 0 us
  other arithmetic: 52 us -> 1.46 us
  waiting for transfers between devices: 55.1 us -> 4.94 us
  starting transfers between devices: 70 us -> 31.8 us
  Pallas kernels: 0 us -> 32.9 us
  local copies, waits for them, and re-layouts: 21.3 us -> 4.18 us
    psum x1 -> x0, blocking collectives: 74.1 us -> none  [shards(): total = lax.psum(local_sum, ('tm', 'tile'))]
    ppermute x26 -> x6, starting transfers between devices: 70 us -> 19.6 us  [the longest x1 5.26 us: shards(): edges_in = lax.ppermute(edges, 'tm', up)]
    ppermute x26 -> x6, waiting for transfers between devices: 55.1 us -> 4.94 us  [the longest x1 4.86 us: shards(): below = lax.ppermute(top, 'tile', backward)]
    pallas_call x0 -> x7, Pallas kernels: none -> 32.9 us  [call(): pl.pallas_call(body, out_shape=out_shape, scratch_shapes=list(scratch), c...]
    add_any x18 -> x0, other arithmetic: 26.8 us -> none  [the longest x6 14.8 us: substep(): later - middle]
    add x16 -> x0, other arithmetic: 15.8 us -> none  [the longest x3 12.9 us: substep(): middle - coeffs[0] * (middle - prior) - coeffs[1] * (later - middle)]
    all_to_all x0 -> x1, starting transfers between devices: none -> 12.1 us  [shards(): parts = lax.all_to_all(partial, ('tm', 'tile'), 0, 0, tiled=True)]
    scatter-add x12 -> x0, local copies, waits for them, and re-layouts: 8.55 us -> none  [the longest x6 4.27 us: adjoint_model(): field = field.at[:, 0].add(beside_all[:, 0])]
  transfers between devices with their start and end apart: 26 -> 7, of which waited for: 11 -> 2; matrix products, arithmetic and copies ran while one was open for 13% -> 0% of each run, Pallas kernels for 0% -> 42%
where the time goes in v1:
time: 78.5 us; the launch traced here: 77.9 us
  Pallas kernels  32.9 us (42%)
  starting transfers between devices  31.8 us (41%)
  waiting for transfers between devices  4.94 us (6%)
  local copies, waits for them, and re-layouts  4.18 us (5%)
  between operations  2.64 us (3%)
  other arithmetic  1.46 us (2%)
    pallas_call x7, Pallas kernels, call(): pl.pallas_call(body, out_shape=out_shape, scratch_shapes=list(scratch), c...  32.9 us
    all_to_all x1, starting transfers between devices, shards(): parts = lax.all_to_all(partial, ('tm', 'tile'), 0, 0, tiled=True)  12.1 us
    ppermute x1, starting transfers between devices, shards(): edges_in = lax.ppermute(edges, 'tm', up)  5.26 us
    ppermute x1, starting transfers between devices, shards(): centre_in = lax.ppermute(centre, 'tm', up)  5.16 us
    ppermute x1, waiting for transfers between devices, shards(): below = lax.ppermute(top, 'tile', backward)  4.86 us
    ppermute x1, starting transfers between devices, shards(): above = lax.ppermute(bottom, 'tile', onward)  4.59 us
    unnamed x36, local copies, waits for them, and re-layouts  4.18 us
    ppermute x1, starting transfers between devices, shards(): below = lax.ppermute(top, 'tile', backward)  2.05 us
  transfers between devices with their start and end apart: 7, of which 2 were waited for; matrix products, arithmetic and copies ran while one was open for 0% of the time, Pallas kernels for 42%

profile of v1, /device:TPU:1, one launch (start us, length us, event | category | flops | bytes accessed | tf_op | source)
XLA Modules:
  0.0 77.9 jit_solution(12962119104799381568)
XLA Ops:
  0.6 1.3 %collective-permute-start.4 = (f32[4,48,1536]{2,1,0:T(8,128)}, f32[4,48,1536]{2,1,0:T(8,128)S(1)}, u32[]{:S(2)}, u32[]{:S(2)}) collective-permute-start(f32[4,48,1536]{2,1,0:T(8,128)} %bitcast.17), channel_id=1, source_target_pairs={{32,0},{64,32},{96,64},{33,1},{65,33},{97,65},{34,2},{66,34},{98,6... | collective-permute-start | bytes 3538952 | tf_op jit(solution)/shard_map/ppermute | solution.py:374
  1.9 0.0 copy-start
  1.9 1.3 %copy-done = f32[1,4,48,1536]{3,2,1,0:T(8,128)S(1)} copy-done((f32[1,4,48,1536]{3,2,1,0:T(8,128)S(1)}, f32[1,4,48,1536]{3,2,1,0:T(8,128)}, u32[]{:S(2)}) %copy-start) | copy-done | bytes 1179672
  3.2 1.3 %copy-done.3 = bf16[1,2,4,48,1536]{4,3,2,1,0:T(8,128)(2,1)S(1)} copy-done((bf16[1,2,4,48,1536]{4,3,2,1,0:T(8,128)(2,1)S(1)}, bf16[1,2,4,48,1536]{4,3,2,1,0:T(8,128)(2,1)}, u32[]{:S(2)}) %copy-start.3) | copy-done | bytes 1179672
  4.5 1.0 %copy-done.5 = s32[48,1536]{1,0:T(8,128)S(1)} copy-done((s32[48,1536]{1,0:T(8,128)S(1)}, s32[48,1536]{1,0:T(8,128)}, u32[]{:S(2)}) %copy-start.5) | copy-done | bytes 294936
  5.4 7.7 %shard_map.111.centre = f32[4,32,1536]{2,1,0:T(8,128)} custom-call(f32[4,48,1536]{2,1,0:T(8,128)S(1)} %bitcast.10, bf16[2,4,48,1536]{3,2,1,0:T(8,128)(2,1)S(1)} %bitcast.23, s32[48,1536]{1,0:T(8,128)S(1)} %copy-done.5), custom_call_target="tpu_custom_call" | custom-call | flops 1000 | bytes 1000 | tf_op jit(solution)/shard_map/pallas_call | solution.py:27
  13.2 0.2 shard_map.112
  13.4 4.6 %collective-permute-start.1 = (f32[104,1536]{1,0:T(8,128)S(1)}, f32[104,1536]{1,0:T(8,128)S(1)}, u32[]{:S(2)}, u32[]{:S(2)}) collective-permute-start(f32[104,1536]{1,0:T(8,128)S(1)} %get-tuple-element.13), channel_id=1, source_target_pairs={{0,1},{1,2},{2,3},{3,4},{4,5},{5,6},{6,7},{7,8},{8,9},{9,10},{10,1... | collective-permute-start | bytes 1916936 | tf_op jit(solution)/shard_map/ppermute | solution.py:378
  18.0 0.0 copy-start.15
  18.0 0.0 copy-start.16
  18.0 0.0 copy-start.17
  18.0 2.1 %collective-permute-start.2 = (f32[104,1536]{1,0:T(8,128)S(1)}, f32[104,1536]{1,0:T(8,128)S(1)}, u32[]{:S(2)}, u32[]{:S(2)}) collective-permute-start(f32[104,1536]{1,0:T(8,128)S(1)} %get-tuple-element.14), channel_id=1, source_target_pairs={{1,0},{2,1},{3,2},{4,3},{5,4},{6,5},{7,6},{8,7},{9,8},{10,9},{11,1... | collective-permute-start | bytes 1916936 | tf_op jit(solution)/shard_map/ppermute | solution.py:379
  20.1 5.2 %collective-permute-start = (f32[4,32,1536]{2,1,0:T(8,128)}, f32[4,32,1536]{2,1,0:T(8,128)}, u32[]{:S(2)}, u32[]{:S(2)}) collective-permute-start(f32[4,32,1536]{2,1,0:T(8,128)} %shard_map.111.centre), channel_id=1, source_target_pairs={{0,32},{32,64},{64,96},{1,33},{33,65},{65,97},{2,34},{34,66},{66,9... | collective-permute-start | bytes 2359304 | tf_op jit(solution)/shard_map/ppermute | solution.py:376
  25.2 0.1 collective-permute-done.1.above
  25.3 4.9 %collective-permute-done.2.below = f32[104,1536]{1,0:T(8,128)S(1)} collective-permute-done((f32[104,1536]{1,0:T(8,128)S(1)}, f32[104,1536]{1,0:T(8,128)S(1)}, u32[]{:S(2)}, u32[]{:S(2)}) %collective-permute-start.2) | collective-permute-done | bytes 639008 | tf_op jit(solution)/shard_map/ppermute | solution.py:379
  30.2 6.4 %shard_map.113 = (f32[4,16,1536]{2,1,0:T(8,128)}, f32[48,1536]{1,0:T(8,128)}) custom-call(f32[4,48,1536]{2,1,0:T(8,128)S(1)} %bitcast.13, bf16[2,4,48,1536]{3,2,1,0:T(8,128)(2,1)S(1)} %bitcast.26, s32[48,1536]{1,0:T(8,128)S(1)} %copy-done.5, f32[104,1536]{1,0:T(8,128)S(1)} %collective-permute-done.1.above, f32[104,1536]{1,0:T(8,128)S(1)} %collective-permute-done.2.below), custom_call_target="tpu_custom_call" | custom-call | flops 1000 | bytes 1000 | tf_op jit(solution)/shard_map/pallas_call | solution.py:27
  36.6 5.3 %collective-permute-start.3 = (f32[4,16,1536]{2,1,0:T(8,128)}, f32[4,16,1536]{2,1,0:T(8,128)}, u32[]{:S(2)}, u32[]{:S(2)}) collective-permute-start(f32[4,16,1536]{2,1,0:T(8,128)} %get-tuple-element.15.edges), channel_id=1, source_target_pairs={{0,32},{32,64},{64,96},{1,33},{33,65},{65,97},{2,34},{34,66},{66,9... | collective-permute-start | bytes 1179656 | tf_op jit(solution)/shard_map/ppermute | solution.py:382
  41.9 1.3 %collective-permute-start.5 = (f32[48,1536]{1,0:T(8,128)}, f32[48,1536]{1,0:T(8,128)}, u32[]{:S(2)}, u32[]{:S(2)}) collective-permute-start(f32[48,1536]{1,0:T(8,128)} %get-tuple-element.18), channel_id=1, source_target_pairs={{32,0},{64,32},{96,64},{33,1},{65,33},{97,65},{34,2},{66,34},{98,6... | collective-permute-start | bytes 884744 | tf_op jit(solution)/shard_map/ppermute | solution.py:383
  43.2 1.7 %shard_map.115 = (f32[1,128]{1,0:T(1,128)}, f32[1,128]{1,0:T(1,128)S(1)}) custom-call(f32[4,48,1536]{2,1,0:T(8,128)S(1)} %bitcast.14, f32[1,128]{1,0:T(1,128)S(1)} %copy-done.15, f32[1,128]{1,0:T(1,128)S(1)} %copy-done.17, s32[1,128]{1,0:T(1,128)S(1)} %copy-done.16), custom_call_target="tpu_custom_call" | custom-call | flops 1000 | bytes 1000 | tf_op jit(solution)/shard_map/pallas_call | solution.py:27
  44.9 0.0 collective-permute-done.4.incoming
  44.9 2.1 %shard_map.117 = f32[128,128]{1,0:T(8,128)S(1)} custom-call(f32[4,48,1536]{2,1,0:T(8,128)S(1)} %bitcast.20, f32[4,48,1536]{2,1,0:T(8,128)S(1)} %bitcast.28, f32[4,48,1536]{2,1,0:T(8,128)S(1)} %bitcast.15, f32[4,48,1536]{2,1,0:T(8,128)S(1)} %collective-permute-done.4.incoming, f32[4,32,1536]{2,1,0:T(8,128)} %shard_map.111.centre, ...), custom_call_target="tpu_custom_call" | custom-call | flops 1000 | bytes 1000 | tf_op jit(solution)/shard_map/pallas_call | solution.py:27
  47.1 0.6 copy-done.14
  47.7 12.1 %all-to-all-start = ((f32[128,1,128]{2,1,0:T(1,128)}), f32[128,1,128]{2,1,0:T(1,128)}, u32[]{:S(2)}, u32[]{:S(2)}) async-start(f32[128,1,128]{2,1,0:T(1,128)} %bitcast.30), calls=%async_computation | async-start | bytes 131072 | tf_op jit(solution)/shard_map/all_to_all | solution.py:386
  59.8 0.0 copy-start.4
  59.9 0.0 copy-start.6
  59.9 0.0 copy-start.9
  59.9 0.0 collective-permute-done.3.edges
  59.9 2.6 %shard_map.114 = f32[4,48,1536]{2,1,0:T(8,128)} custom-call(f32[4,48,1536]{2,1,0:T(8,128)S(1)} %bitcast.29, f32[4,48,1536]{2,1,0:T(8,128)S(1)} %bitcast.21, f32[4,48,1536]{2,1,0:T(8,128)S(1)} %bitcast.16, f32[4,32,1536]{2,1,0:T(8,128)} %collective-permute-done.centre, f32[4,16,1536]{2,1,0:T(8,128)} %collective-permute-done.3.edges), custom_call_target="tpu_custom_call" | custom-call | flops 1000 | bytes 1000 | tf_op jit(solution)/shard_map/pallas_call | solution.py:27
  62.5 0.0 collective-permute-done.5.rims
  62.6 12.1 %shard_map.116 = f32[4,48,1536]{2,1,0:T(8,128)} custom-call(f32[4,48,1536]{2,1,0:T(8,128)S(1)} %copy-done.9, f32[48,1536]{1,0:T(8,128)} %collective-permute-done.5.rims, bf16[2,4,48,1536]{3,2,1,0:T(8,128)(2,1)S(1)} %bitcast.27, s32[48,1536]{1,0:T(8,128)S(1)} %copy-done.6, f32[104,1536]{1,0:T(8,128)S(1)} %copy-done.11, f32[104,1536]{1,0:T(8,128)S(1)} %copy-done.13, ...), custom_call_target="tpu_custom_call" | custom-call | flops 1000 | bytes 1000 | tf_op jit(solution)/shard_map/pallas_call | solution.py:27
  74.7 0.0 all-to-all-done
  74.7 1.5 %slice_reduce_fusion = f32[]{:T(128)} fusion(f32[128,128]{1,0:T(8,128)} %bitcast.8), kind=kLoop, calls=%fused_computation | loop fusion | flops 127 | bytes 516 | tf_op jit(solution)/shard_map/reduce_sum | solution.py:390
  (26 shorter events, 0.1 us)
Async XLA Ops:
  0.6 44.3 %collective-permute-start.4 = (f32[4,48,1536]{2,1,0:T(8,128)}, f32[4,48,1536]{2,1,0:T(8,128)S(1)}, u32[]{:S(2)}, u32[]{:S(2)}) collective-permute-start(f32[4,48,1536]{2,1,0:T(8,128)} %bitcast.17), channel_id=1, source_target_pairs={{32,0},{64,32},{96,64},{33,1},{65,33},{97,65},{34,2},{66,34},{98,6... | collective-permute-start | bytes 3538952 | tf_op jit(solution)/shard_map/ppermute | solution.py:374
  1.9 1.3 %copy-start = (f32[1,4,48,1536]{3,2,1,0:T(8,128)S(1)}, f32[1,4,48,1536]{3,2,1,0:T(8,128)}, u32[]{:S(2)}) copy-start(f32[1,4,48,1536]{3,2,1,0:T(8,128)} %param.10) | copy-start | bytes 3538948
  3.2 1.3 %copy-start.3 = (bf16[1,2,4,48,1536]{4,3,2,1,0:T(8,128)(2,1)S(1)}, bf16[1,2,4,48,1536]{4,3,2,1,0:T(8,128)(2,1)}, u32[]{:S(2)}) copy-start(bf16[1,2,4,48,1536]{4,3,2,1,0:T(8,128)(2,1)} %param.13) | copy-start | bytes 3538948
  4.5 1.0 %copy-start.5 = (s32[48,1536]{1,0:T(8,128)S(1)}, s32[48,1536]{1,0:T(8,128)}, u32[]{:S(2)}) copy-start(s32[48,1536]{1,0:T(8,128)} %wake.5) | copy-start | bytes 884740
  5.4 7.7 %copy-start.2 = (f32[1,4,48,1536]{3,2,1,0:T(8,128)S(1)}, f32[1,4,48,1536]{3,2,1,0:T(8,128)}, u32[]{:S(2)}) copy-start(f32[1,4,48,1536]{3,2,1,0:T(8,128)} %param.8) | copy-start | bytes 3538948
  13.4 11.9 %collective-permute-start.1 = (f32[104,1536]{1,0:T(8,128)S(1)}, f32[104,1536]{1,0:T(8,128)S(1)}, u32[]{:S(2)}, u32[]{:S(2)}) collective-permute-start(f32[104,1536]{1,0:T(8,128)S(1)} %get-tuple-element.13), channel_id=1, source_target_pairs={{0,1},{1,2},{2,3},{3,4},{4,5},{5,6},{6,7},{7,8},{8,9},{9,10},{10,1... | collective-permute-start | bytes 1916936 | tf_op jit(solution)/shard_map/ppermute | solution.py:378
  18.0 25.2 %copy-start.15 = (f32[1,128]{1,0:T(1,128)S(1)}, f32[1,128]{1,0:T(1,128)}, u32[]{:S(2)}) copy-start(f32[1,128]{1,0:T(1,128)} %dual.3) | copy-start | bytes 1540
  18.0 25.2 %copy-start.16 = (s32[1,128]{1,0:T(1,128)S(1)}, s32[1,128]{1,0:T(1,128)}, u32[]{:S(2)}) copy-start(s32[1,128]{1,0:T(1,128)} %cell.3) | copy-start | bytes 1540
  18.0 25.1 %copy-start.17 = (f32[1,128]{1,0:T(1,128)S(1)}, f32[1,128]{1,0:T(1,128)}, u32[]{:S(2)}) copy-start(f32[1,128]{1,0:T(1,128)} %var.1) | copy-start | bytes 1540
  18.0 12.2 %collective-permute-start.2 = (f32[104,1536]{1,0:T(8,128)S(1)}, f32[104,1536]{1,0:T(8,128)S(1)}, u32[]{:S(2)}, u32[]{:S(2)}) collective-permute-start(f32[104,1536]{1,0:T(8,128)S(1)} %get-tuple-element.14), channel_id=1, source_target_pairs={{1,0},{2,1},{3,2},{4,3},{5,4},{6,5},{7,6},{8,7},{9,8},{10,9},{11,1... | collective-permute-start | bytes 1916936 | tf_op jit(solution)/shard_map/ppermute | solution.py:379
  20.1 39.8 %collective-permute-start = (f32[4,32,1536]{2,1,0:T(8,128)}, f32[4,32,1536]{2,1,0:T(8,128)}, u32[]{:S(2)}, u32[]{:S(2)}) collective-permute-start(f32[4,32,1536]{2,1,0:T(8,128)} %shard_map.111.centre), channel_id=1, source_target_pairs={{0,32},{32,64},{64,96},{1,33},{33,65},{65,97},{2,34},{34,66},{66,9... | collective-permute-start | bytes 2359304 | tf_op jit(solution)/shard_map/ppermute | solution.py:376
  25.3 11.3 %copy-start.10 = (f32[104,1536]{1,0:T(8,128)}, f32[104,1536]{1,0:T(8,128)S(1)}, u32[]{:S(2)}) copy-start(f32[104,1536]{1,0:T(8,128)S(1)} %collective-permute-done.1.above) | copy-start | bytes 1916932
  30.2 6.4 %copy-start.12 = (f32[104,1536]{1,0:T(8,128)}, f32[104,1536]{1,0:T(8,128)S(1)}, u32[]{:S(2)}) copy-start(f32[104,1536]{1,0:T(8,128)S(1)} %collective-permute-done.2.below) | copy-start | bytes 1916932
  36.6 8.3 %copy-start.7 = (f32[1,4,48,1536]{3,2,1,0:T(8,128)S(1)}, f32[1,4,48,1536]{3,2,1,0:T(8,128)}, u32[]{:S(2)}) copy-start(f32[1,4,48,1536]{3,2,1,0:T(8,128)} %param.11) | copy-start | bytes 3538948
  36.6 23.3 %collective-permute-start.3 = (f32[4,16,1536]{2,1,0:T(8,128)}, f32[4,16,1536]{2,1,0:T(8,128)}, u32[]{:S(2)}, u32[]{:S(2)}) collective-permute-start(f32[4,16,1536]{2,1,0:T(8,128)} %get-tuple-element.15.edges), channel_id=1, source_target_pairs={{0,32},{32,64},{64,96},{1,33},{33,65},{65,97},{2,34},{34,66},{66,9... | collective-permute-start | bytes 1179656 | tf_op jit(solution)/shard_map/ppermute | solution.py:382
  41.9 20.7 %collective-permute-start.5 = (f32[48,1536]{1,0:T(8,128)}, f32[48,1536]{1,0:T(8,128)}, u32[]{:S(2)}, u32[]{:S(2)}) collective-permute-start(f32[48,1536]{1,0:T(8,128)} %get-tuple-element.18), channel_id=1, source_target_pairs={{32,0},{64,32},{96,64},{33,1},{65,33},{97,65},{34,2},{66,34},{98,6... | collective-permute-start | bytes 884744 | tf_op jit(solution)/shard_map/ppermute | solution.py:383
  44.9 2.2 %copy-start.8 = (f32[4,48,1536]{2,1,0:T(8,128)}, f32[4,48,1536]{2,1,0:T(8,128)S(1)}, u32[]{:S(2)}) copy-start(f32[4,48,1536]{2,1,0:T(8,128)S(1)} %collective-permute-done.4.incoming) | copy-start | bytes 3538948
  44.9 15.0 %copy-start.1 = (f32[1,4,48,1536]{3,2,1,0:T(8,128)S(1)}, f32[1,4,48,1536]{3,2,1,0:T(8,128)}, u32[]{:S(2)}) copy-start(f32[1,4,48,1536]{3,2,1,0:T(8,128)} %param.10) | copy-start | bytes 3538948
  47.1 0.6 copy-start.14
  47.7 27.0 %all-to-all-start = ((f32[128,1,128]{2,1,0:T(1,128)}), f32[128,1,128]{2,1,0:T(1,128)}, u32[]{:S(2)}, u32[]{:S(2)}) async-start(f32[128,1,128]{2,1,0:T(1,128)} %bitcast.30), calls=%async_computation | async-start | bytes 131072 | tf_op jit(solution)/shard_map/all_to_all | solution.py:386
  59.8 2.7 %copy-start.4 = (bf16[1,2,4,48,1536]{4,3,2,1,0:T(8,128)(2,1)S(1)}, bf16[1,2,4,48,1536]{4,3,2,1,0:T(8,128)(2,1)}, u32[]{:S(2)}) copy-start(bf16[1,2,4,48,1536]{4,3,2,1,0:T(8,128)(2,1)} %param.13) | copy-start | bytes 3538948
  59.9 2.7 %copy-start.6 = (s32[48,1536]{1,0:T(8,128)S(1)}, s32[48,1536]{1,0:T(8,128)}, u32[]{:S(2)}) copy-start(s32[48,1536]{1,0:T(8,128)} %wake.5) | copy-start | bytes 884740
  59.9 2.7 %copy-start.9 = (f32[4,48,1536]{2,1,0:T(8,128)S(1)}, f32[4,48,1536]{2,1,0:T(8,128)}, u32[]{:S(2)}) copy-start(f32[4,48,1536]{2,1,0:T(8,128)} %copy-done.8) | copy-start | bytes 3538948
  59.9 2.7 %copy-start.11 = (f32[104,1536]{1,0:T(8,128)S(1)}, f32[104,1536]{1,0:T(8,128)}, u32[]{:S(2)}) copy-start(f32[104,1536]{1,0:T(8,128)} %copy-done.10) | copy-start | bytes 1916932
  59.9 2.7 %copy-start.13 = (f32[104,1536]{1,0:T(8,128)S(1)}, f32[104,1536]{1,0:T(8,128)}, u32[]{:S(2)}) copy-start(f32[104,1536]{1,0:T(8,128)} %copy-done.12) | copy-start | bytes 1916932

commit v2 on v0

v2 whole, which is shorter than its diff:
```python
import functools

import jax
import jax.numpy as jnp
from jax import lax
from jax.experimental import pallas as pl
from jax.experimental.pallas import tpu as pltpu
from jax.sharding import PartitionSpec as P

SUB = 6
LANES = 128
KAPPA = 0.04
MIX = 0.05
BASE = 16
INC, WIND, KD, MULT = 0, 4, 12, 13
CHANNELS = 17
WEIGHTS = 5
MIB = 2**20
ANY = pl.BlockSpec(memory_space=pl.ANY)
VMEM = pl.BlockSpec(memory_space=pltpu.VMEM)


def call(body, out_shape, *args, scratch=(), vmem=16, flops=1000, **kwargs):
    return pl.pallas_call(
        body,
        out_shape=out_shape,
        scratch_shapes=list(scratch),
        compiler_params=pltpu.CompilerParams(vmem_limit_bytes=vmem * MIB),
        cost_estimate=pl.CostEstimate(flops=flops, bytes_accessed=1000, transcendentals=0),
        **kwargs,
    )(*args)


def in_hbm(*values):
    return [pltpu.with_memory_space_constraint(value, pltpu.HBM) for value in values]


def to_hbm(*shape):
    return pltpu.HBM(shape, jnp.float32)


def in_vmem(*shape):
    return pltpu.VMEM(shape, jnp.float32)


def f32(*shape):
    return jax.ShapeDtypeStruct(shape, jnp.float32)


def cols(j):
    return pl.ds(j * LANES, LANES)


def diffusion_of(wake):
    return KAPPA * (1.0 + 2.0 * wake.astype(jnp.float32))


def edge_lanes(rows):
    lane = lax.broadcasted_iota(jnp.int32, (rows, LANES), 1)
    return lane == 0, lane == LANES - 1, jnp.zeros((rows, LANES), jnp.float32)


def put_weights(coef, wind_at, kd_at, level, row, rows, transpose):
    columns = coef[0].shape[1]
    first, last, zero = edge_lanes(rows)

    def weights(j):
        u, v = wind_at(0, level, j), wind_at(1, level, j)
        kd = kd_at(j)
        south = kd - jnp.minimum(u, 0.0)
        east = kd - jnp.minimum(v, 0.0)
        return jnp.maximum(u, 0.0) + kd, south, jnp.maximum(v, 0.0) + kd, east

    here = pl.ds(row, rows)
    before, now = zero, weights(0)
    for j in range(columns):
        after = weights(j + 1) if j + 1 < columns else (zero,) * 4
        north, south, west, east = now
        coef[0][level, j, here, :] = (1.0 - 2.0 * MIX) - ((north + south) + (west + east))
        coef[1][level, j, here, :] = north
        coef[2][level, j, here, :] = south
        if transpose:
            coef[3][level, j, here, :] = pltpu.roll(jnp.where(last, before, east), 1, 1)
            coef[4][level, j, here, :] = pltpu.roll(jnp.where(first, after[2], west), LANES - 1, 1)
        else:
            coef[3][level, j, here, :] = west
            coef[4][level, j, here, :] = east
        before, now = east, after


FORWARD = ((0, 0), (1, 0), (2, 0), (3, 0), (4, 0))
TRANSPOSE = ((0, 0), (2, -1), (1, 1), (3, 0), (4, 0))


def strip_weights(coef, wind_v, wake_v, level, transpose):
    def rows_of(tile, carry):
        here = pl.ds(pl.multiple_of(tile * 16, 16), 16)
        put_weights(
            coef,
            lambda part, level, j: wind_v[part, level, here, cols(j)].astype(jnp.float32),
            lambda j: diffusion_of(wake_v[here, cols(j)]),
            level, BASE + tile * 16, 16, transpose,
        )
        return carry

    lax.fori_loop(0, wake_v.shape[0] // 16, rows_of, 0)


def halo_weights(coef, halo, level, row, transpose):
    levels = coef[0].shape[0]
    put_weights(
        coef,
        lambda part, level, j: halo[pl.ds((WIND + part * levels + level) * SUB, SUB), cols(j)],
        lambda j: halo[pl.ds(KD * SUB, SUB), cols(j)],
        level, row, SUB, transpose,
    )


def update(src, dst, coef, table, start, tiles):
    levels, columns = src.shape[0], src.shape[1]
    first, last, zero = edge_lanes(8)
    rows = [start + 8 * tile for tile in range(tiles)]
    blank = [[zero] * levels] * tiles

    def load(j):
        return [[src[level, j, pl.ds(row, 8), :] for level in range(levels)] for row in rows]

    before, now = blank, load(0)
    for j in range(columns):
        after = load(j + 1) if j + 1 < columns else blank
        for row, west, here, east in zip(rows, before, now, after):
            for level in range(levels):

                def weight(k):
                    which, shift = table[k]
                    return coef[which][level, j, pl.ds(row + shift, 8), :]

                middle = here[level]
                total = weight(0) * middle
                total += weight(1) * src[level, j, pl.ds(row - 1, 8), :]
                total += weight(2) * src[level, j, pl.ds(row + 1, 8), :]
                total += weight(3) * pltpu.roll(jnp.where(last, west[level], middle), 1, 1)
                total += weight(4) * pltpu.roll(jnp.where(first, east[level], middle), LANES - 1, 1)
                if level == 0:
                    vertical = here[1]
                elif level == levels - 1:
                    vertical = here[level - 1]
                else:
                    vertical = here[level - 1] + here[level + 1]
                dst[level, j, pl.ds(row, 8), :] = total + MIX * vertical
        before, now = now, after


def run_model(a, b, coef, table, rows):
    def tiles(reach):
        return -(-(rows + 2 * reach) // 8)

    update(a, b, coef, table, BASE - (SUB - 1), tiles(SUB - 1))

    def pair(i, carry):
        update(b, a, coef, table, BASE - (SUB - 2) + 2 * i, tiles(SUB - 2))
        update(a, b, coef, table, BASE - (SUB - 3) + 2 * i, tiles(SUB - 3))
        return carry

    lax.fori_loop(0, (SUB - 2) // 2, pair, 0)
    update(b, a, coef, table, BASE, tiles(0))


def pack_kernel(inc, mult, winds, wake, top, bottom, inc_v, mult_v, wind_v, wake_v, sems):
    levels, rows, columns = inc.shape
    copies = []
    for side, (row, row16) in enumerate(((0, 0), (rows - 8, rows - 16))):
        copies.append(
            [
                pltpu.make_async_copy(inc.at[:, pl.ds(row, 8), :], inc_v.at[side], sems.at[side, 0]),
                pltpu.make_async_copy(mult.at[:, pl.ds(row, 8), :], mult_v.at[side], sems.at[side, 1]),
                pltpu.make_async_copy(winds.at[:, :, pl.ds(row16, 16), :], wind_v.at[side], sems.at[side, 2]),
                pltpu.make_async_copy(wake.at[pl.ds(row, 8), :], wake_v.at[side], sems.at[side, 3]),
            ]
        )
    for copy in copies[0] + copies[1]:
        copy.start()
    for side, (out, at, at16) in enumerate(((top, 0, 0), (bottom, 8 - SUB, 16 - SUB))):
        for copy in copies[side]:
            copy.wait()
        for level in range(levels):
            out[pl.ds((INC + level) * SUB, SUB), :] = inc_v[side, level, at : at + SUB, :]
            out[pl.ds((MULT + level) * SUB, SUB), :] = mult_v[side, level, at : at + SUB, :]
            for part in range(2):
                wind = wind_v[side, part, level].astype(jnp.float32)
                out[pl.ds((WIND + part * levels + level) * SUB, SUB), :] = wind[at16 : at16 + SUB]
        out[pl.ds(KD * SUB, SUB), :] = diffusion_of(wake_v[side, at : at + SUB, :])
        out[pl.ds(CHANNELS * SUB, 2), :] = jnp.zeros((2, columns), jnp.float32)


def pack(inc, mult, winds, wake):
    levels, rows, columns = inc.shape
    message = in_vmem(CHANNELS * SUB + 2, columns)
    return call(
        pack_kernel,
        [message, message],
        *in_hbm(inc, mult, winds, wake),
        in_specs=[ANY] * 4,
        scratch=[
            pltpu.VMEM((2, levels, 8, columns), jnp.float32),
            pltpu.VMEM((2, levels, 8, columns), jnp.float32),
            pltpu.VMEM((2, 2, levels, 16, columns), jnp.bfloat16),
            pltpu.VMEM((2, 8, columns), jnp.int32),
            pltpu.SemaphoreType.DMA((2, 4)),
        ],
        vmem=6,
    )


def one_hots(cell, rows, columns):
    where = lax.broadcasted_iota(jnp.int32, (rows, LANES), 0) * columns
    offset = cell - where
    in_row = (offset >= 0) & (offset < columns)
    column = jnp.sum(jnp.where(in_row, offset, 0), axis=0, keepdims=True)
    in_column = lax.broadcasted_iota(jnp.int32, (columns, LANES), 0) == column
    return in_row, jnp.where(in_column, 1.0, 0.0).astype(jnp.bfloat16)


def three_parts(x):
    high = x.astype(jnp.bfloat16)
    rest = x - high.astype(jnp.float32)
    middle = rest.astype(jnp.bfloat16)
    return high, middle, (rest - middle.astype(jnp.float32)).astype(jnp.bfloat16)


def local_kernel(
    inc, mult, var, winds, wake, dual, obs_var, cell,
    out_obs, inc_base, mult_base, acc, field, *rest,
):
    coef, rest = rest[:WEIGHTS], rest[WEIGHTS:]
    inc_v, mult_v, var_v, wind_v, wake_v, in_sem, wind_sem, wake_sem, out_sem = rest
    levels, rows, columns = inc.shape
    tiles = columns // LANES
    wind_copies = [
        [pltpu.make_async_copy(winds.at[part, level], wind_v.at[part, level], wind_sem.at[part, level]) for part in range(2)]
        for level in range(levels)
    ]
    wake_copy = pltpu.make_async_copy(wake, wake_v, wake_sem)
    fetch = [
        [pltpu.make_async_copy(x.at[level], v.at[level], in_sem.at[k, level]) for level in range(levels)]
        for k, (x, v) in enumerate(((inc, inc_v), (mult, mult_v), (var, var_v)))
    ]
    wake_copy.start()
    for copy in [c for pair in wind_copies for c in pair] + [c for copies in fetch for c in copies]:
        copy.start()
    in_row, in_column = one_hots(cell[...], levels * rows, columns)
    spread = lax.dot_general(
        jnp.concatenate(three_parts(jnp.where(in_row, dual[...], 0.0)), axis=1),
        jnp.concatenate([in_column] * 3, axis=1),
        (((1,), (1,)), ((), ())),
        preferred_element_type=jnp.float32,
    )
    wake_copy.wait()
    for level in range(levels):
        for copy in wind_copies[level]:
            copy.wait()
        strip_weights(coef, wind_v, wake_v, level, False)
    for copy in fetch[0]:
        copy.wait()
    picked = jnp.zeros((levels * rows, LANES), jnp.float32)
    for part in three_parts(inc_v[...].reshape(levels * rows, columns)):
        picked += jnp.dot(part, in_column, preferred_element_type=jnp.float32)
    sampled = jnp.sum(jnp.where(in_row, picked, 0.0), axis=0, keepdims=True)
    value = obs_var[...] * dual[...] + sampled
    out_obs[...] = value
    total = jnp.zeros((8, columns), jnp.float32)
    results = []
    for level in range(levels):
        fetch[1][level].wait()
        fetch[2][level].wait()
        for row in range(0, rows, 8):
            here = pl.ds(row, 8)
            m, q = mult_v[level, here, :], inc_v[level, here, :]
            at = level * rows + row
            weighted = var_v[level, here, :] * m + q
            total += m * (weighted + q)
            mult_v[level, here, :] = m + spread[at : at + 8]
            var_v[level, here, :] = weighted
            for j in range(tiles):
                field[level, j, pl.ds(BASE + row, 8), :] = q[:, j * LANES : (j + 1) * LANES]
        for k, (v, x) in enumerate(((mult_v, inc_base), (var_v, mult_base))):
            results.append(pltpu.make_async_copy(v.at[level], x.at[level], out_sem.at[k, level]))
            results[-1].start()
    total = sum(total[:, j * LANES : (j + 1) * LANES] for j in range(tiles))
    first = lax.broadcasted_iota(jnp.int32, (8, LANES), 0) == 0
    acc[...] = total + jnp.where(first, dual[...] * (value + sampled), 0.0)
    for copy in results:
        copy.wait()


def local(inc, mult, var, winds, wake, dual, obs_var, cell):
    levels, rows, columns = inc.shape
    strip = to_hbm(levels, rows, columns)
    field = (levels, columns // LANES, rows + 2 * BASE, LANES)
    return call(
        local_kernel,
        [f32(*dual.shape), strip, strip, in_vmem(8, LANES)] + [in_vmem(*field)] * (1 + WEIGHTS),
        *in_hbm(inc, mult, var, winds, wake), dual, obs_var, cell,
        in_specs=[ANY] * 5 + [VMEM] * 3,
        out_specs=[VMEM, ANY, ANY] + [VMEM] * (2 + WEIGHTS),
        scratch=[pltpu.VMEM(inc.shape, jnp.float32)] * 3
        + [
            pltpu.VMEM(winds.shape, jnp.bfloat16),
            pltpu.VMEM(wake.shape, jnp.int32),
            pltpu.SemaphoreType.DMA((3, levels)),
            pltpu.SemaphoreType.DMA((2, levels)),
            pltpu.SemaphoreType.DMA,
            pltpu.SemaphoreType.DMA((2, levels)),
        ],
        vmem=12,
        flops=10**11,
    )


def forward_kernel(*refs):
    above, below, moved, rims, above_out, below_out, a = refs[1 + WEIGHTS : 8 + WEIGHTS]
    coef, (b, sems) = refs[8 + WEIGHTS : -2], refs[-2:]
    levels, rows, columns = moved.shape
    tiles = columns // LANES
    copies = [
        pltpu.make_async_copy(above, above_out, sems.at[0]),
        pltpu.make_async_copy(below, below_out, sems.at[1]),
    ]
    for copy in copies:
        copy.start()
    for halo, row, at in ((above, BASE - SUB, 0), (below, BASE + rows, levels)):
        for level in range(levels):
            halo_weights(coef, halo, level, row, False)
            rims[pl.ds((at + level) * SUB, SUB), :] = halo[pl.ds((MULT + level) * SUB, SUB), :]
            for j in range(tiles):
                a[level, j, pl.ds(row, SUB), :] = halo[pl.ds((INC + level) * SUB, SUB), cols(j)]
    run_model(a, b, coef, FORWARD, rows)
    for level in range(levels):
        for j in range(tiles):
            moved[level, :, cols(j)] = a[level, j, pl.ds(BASE, rows), :]
    for copy in copies:
        copy.wait()


def forward(field, coef, above, below, rows):
    levels, tiles = field.shape[:2]
    return call(
        forward_kernel,
        [
            in_vmem(levels, rows, tiles * LANES),
            in_vmem(2 * levels * SUB, tiles * LANES),
            to_hbm(*above.shape),
            to_hbm(*below.shape),
        ]
        + [in_vmem(*field.shape)] * (1 + WEIGHTS),
        field, *coef, above, below,
        in_specs=[VMEM] * (3 + WEIGHTS),
        out_specs=[VMEM, VMEM, ANY, ANY] + [VMEM] * (1 + WEIGHTS),
        input_output_aliases={i: i + 4 for i in range(1 + WEIGHTS)},
        scratch=[pltpu.VMEM(field.shape, jnp.float32), pltpu.SemaphoreType.DMA((2,))],
        vmem=4,
    )


def sums_kernel(moved, incoming, acc, out):
    levels, rows, columns = moved.shape
    total = jnp.zeros((8, columns), jnp.float32)
    for level in range(levels):
        for row in range(0, rows, 8):
            here = pl.ds(row, 8)
            total += moved[level, here, :] * incoming[level, here, :]
    total = sum(total[:, j * LANES : (j + 1) * LANES] for j in range(columns // LANES))
    out[...] = jnp.full(out.shape, jnp.sum(acc[...] - 2.0 * total), jnp.float32)


def sums(count, moved, incoming, acc):
    return call(sums_kernel, f32(count, LANES), moved, incoming, acc, vmem=6)


def adjoint_kernel(
    incoming, rims, inc_base, winds, wake, above, below, out,
    a, b, base_v, wind_v, wake_v, halo_v, wind_sem, base_sem, sems, *coef,
):
    levels, rows, columns = incoming.shape
    tiles = columns // LANES
    wake_copy = pltpu.make_async_copy(wake, wake_v, sems.at[0])
    winds_copies = [
        [pltpu.make_async_copy(winds.at[part, level], wind_v.at[part, level], wind_sem.at[part, level]) for part in range(2)]
        for level in range(levels)
    ]
    halos = [
        pltpu.make_async_copy(x, halo_v.at[k], sems.at[1 + k]) for k, x in enumerate((above, below))
    ]
    bases = [
        pltpu.make_async_copy(inc_base.at[level], base_v.at[level], base_sem.at[level])
        for level in range(levels)
    ]
    wake_copy.start()
    for copy in [c for pair in winds_copies for c in pair] + halos + bases:
        copy.start()
    for level in range(levels):
        for j in range(tiles):
            a[level, j, pl.ds(BASE, rows), :] = incoming[level, :, cols(j)]
            for row, at in ((BASE - SUB, level), (BASE + rows, levels + level)):
                a[level, j, pl.ds(row, SUB), :] = rims[pl.ds(at * SUB, SUB), cols(j)]
    wake_copy.wait()
    for level in range(levels):
        for copy in winds_copies[level]:
            copy.wait()
        strip_weights(coef, wind_v, wake_v, level, True)
    for copy in halos:
        copy.wait()
    for k, row in enumerate((BASE - SUB, BASE + rows)):
        for level in range(levels):
            halo_weights(coef, halo_v.at[k], level, row, True)
    run_model(a, b, coef, TRANSPOSE, rows)
    copies = []
    for level in range(levels):
        bases[level].wait()
        for j in range(tiles):
            base_v[level, :, cols(j)] -= a[level, j, pl.ds(BASE, rows), :]
        copies.append(pltpu.make_async_copy(base_v.at[level], out.at[level], base_sem.at[level]))
        copies[-1].start()
    for copy in copies:
        copy.wait()


def adjoint(incoming, rims, inc_base, winds, wake, above, below):
    levels, rows, columns = incoming.shape
    field = (levels, columns // LANES, rows + 2 * BASE, LANES)
    return call(
        adjoint_kernel,
        to_hbm(*incoming.shape),
        incoming, rims, *in_hbm(inc_base, winds, wake, above, below),
        in_specs=[VMEM] * 2 + [ANY] * 5,
        out_specs=ANY,
        scratch=[
            pltpu.VMEM(field, jnp.float32),
            pltpu.VMEM(field, jnp.float32),
            pltpu.VMEM(incoming.shape, jnp.float32),
            pltpu.VMEM(winds.shape, jnp.bfloat16),
            pltpu.VMEM(wake.shape, jnp.int32),
            pltpu.VMEM((2,) + above.shape, jnp.float32),
            pltpu.SemaphoreType.DMA((2, levels)),
            pltpu.SemaphoreType.DMA((levels,)),
            pltpu.SemaphoreType.DMA((3,)),
        ]
        + [pltpu.VMEM(field, jnp.float32)] * WEIGHTS,
        vmem=28,
    )


def finish_kernel(base, moved, parts, out, curvature, base_v, parts_v, sems, *, elements):
    levels = base.shape[0]
    fetch = [
        pltpu.make_async_copy(base.at[level], base_v.at[level], sems.at[level])
        for level in range(levels)
    ]
    fetch_parts = pltpu.make_async_copy(parts, parts_v, sems.at[levels])
    for copy in fetch + [fetch_parts]:
        copy.start()
    copies = []
    for level in range(levels):
        fetch[level].wait()
        base_v[level] -= moved[level]
        copies.append(pltpu.make_async_copy(base_v.at[level], out.at[level], sems.at[level]))
        copies[-1].start()
    fetch_parts.wait()
    total = jnp.sum(parts_v[...], axis=0, keepdims=True)[:, :1]
    curvature[...] = total / jnp.float32(elements)
    for copy in copies:
        copy.wait()


def finish(base, moved, parts, elements):
    levels = base.shape[0]
    base, parts = in_hbm(base, parts)
    return call(
        functools.partial(finish_kernel, elements=elements),
        [to_hbm(*base.shape), f32(1, 1)],
        base, moved, parts,
        in_specs=[ANY, VMEM, ANY],
        out_specs=[ANY, VMEM],
        scratch=[
            pltpu.VMEM(base.shape, jnp.float32),
            pltpu.VMEM(parts.shape, jnp.float32),
            pltpu.SemaphoreType.DMA((levels + 1,)),
        ],
        vmem=6,
    )


def shards(multiplier, obs_dual, increment, error_var, obs_var, winds, wake, cell):
    mult, inc, var, wind = multiplier[0], increment[0], error_var[0], winds[0]
    windows, strips = lax.axis_size("tm"), lax.axis_size("tile")
    count = windows * strips
    up = [(k, k + 1) for k in range(windows - 1)]
    down = [(k + 1, k) for k in range(windows - 1)]
    onward = [(t, t + 1) for t in range(strips - 1)]
    backward = [(t + 1, t) for t in range(strips - 1)]

    incoming = lax.ppermute(mult, "tm", down)
    top, bottom = pack(inc, mult, wind, wake)
    above = lax.ppermute(bottom, "tile", onward)
    below = lax.ppermute(top, "tile", backward)
    inc, top = lax.optimization_barrier((inc, top))
    out_obs, inc_base, mult_base, acc, field, *coef = local(
        inc, mult, var, wind, wake, obs_dual, obs_var, cell
    )
    moved, rims, above, below, *_ = forward(field, coef, above, below, inc.shape[1])
    moved_in = lax.ppermute(moved, "tm", up)
    rims_in = lax.ppermute(rims, "tm", down)
    partial = sums(count, moved, incoming, acc)
    parts = lax.all_to_all(partial, ("tm", "tile"), 0, 0, tiled=True)
    out_inc = adjoint(incoming, rims_in, inc_base, wind, wake, above, below)
    elements = count * (2 * inc.size + obs_dual.shape[1])
    out_mult, curvature = finish(mult_base, moved_in, parts, elements)
    return out_mult[None], out_obs, out_inc[None], curvature[0, 0]


def solution(mesh):
    return jax.shard_map(
        shards,
        mesh=mesh,
        in_specs=(
            P("tm", None, "tile", None),
            P("tm", "tile"),
            P("tm", None, "tile", None),
            P("tm", None, "tile", None),
            P("tm", "tile"),
            P("tm", None, None, "tile", None),
            P("tile", None),
            P("tm", "tile"),
        ),
        out_specs=(P("tm", None, "tile", None), P("tm", "tile"), P("tm", None, "tile", None), P()),
        check_vma=False,
    )
```

time: 279 us -> 63.1 us (0.23)
  the two profiles are of different devices: /device:TPU:1 before, /device:TPU:24 now
where the time goes in v2:
time: 63.1 us; the launch traced here: 62.8 us
  Pallas kernels  27.9 us (44%)
  starting transfers between devices  24.9 us (39%)
  waiting for transfers between devices  8.46 us (13%)
  between operations  0.95 us (2%)
    pallas_call x6, Pallas kernels, call(): pl.pallas_call(body, out_shape=out_shape, scratch_shapes=list(scratch), c...  27.9 us
    all_to_all x1, starting transfers between devices, shards(): parts = lax.all_to_all(partial, ('tm', 'tile'), 0, 0, tiled=True)  13.3 us
    ppermute x1, starting transfers between devices, shards(): moved_in = lax.ppermute(moved, 'tm', up)  4.53 us
    all_to_all x1, waiting for transfers between devices, shards(): parts = lax.all_to_all(partial, ('tm', 'tile'), 0, 0, tiled=True)  4.21 us
    ppermute x1, waiting for transfers between devices, shards(): above = lax.ppermute(bottom, 'tile', onward)  3.5 us
    ppermute x1, starting transfers between devices, shards(): above = lax.ppermute(bottom, 'tile', onward)  2.24 us
    ppermute x1, starting transfers between devices, shards(): below = lax.ppermute(top, 'tile', backward)  2.09 us
    ppermute x1, starting transfers between devices, shards(): incoming = lax.ppermute(mult, 'tm', down)  1.42 us
  transfers between devices with their start and end apart: 6, of which 3 were waited for; matrix products, arithmetic and copies ran while one was open for 0% of the time, Pallas kernels for 40%

profile of v2, /device:TPU:24, one launch (start us, length us, event | category | flops | bytes accessed | tf_op | source)
XLA Modules:
  0.0 62.8 jit_solution(3043595172280296058)
XLA Ops:
  0.6 0.0 copy-start.2
  0.6 0.0 copy-start.3
  0.7 0.0 copy-start.1
  0.7 1.4 %collective-permute-start.3 = (f32[4,48,1536]{2,1,0:T(8,128)}, f32[4,48,1536]{2,1,0:T(8,128)S(1)}, u32[]{:S(2)}, u32[]{:S(2)}) collective-permute-start(f32[4,48,1536]{2,1,0:T(8,128)} %bitcast.18), channel_id=1, source_target_pairs={{32,0},{64,32},{96,64},{33,1},{65,33},{97,65},{34,2},{66,34},{98,6... | collective-permute-start | bytes 3538952 | tf_op jit(solution)/shard_map/ppermute | solution.py:502
  2.1 1.6 %shard_map.111 = (f32[104,1536]{1,0:T(8,128)S(1)}, f32[104,1536]{1,0:T(8,128)S(1)}) custom-call(f32[4,48,1536]{2,1,0:T(8,128)} %bitcast.16, f32[4,48,1536]{2,1,0:T(8,128)} %bitcast.19, bf16[2,4,48,1536]{3,2,1,0:T(8,128)(2,1)} %bitcast.12, s32[48,1536]{1,0:T(8,128)} %wake.5), custom_call_target="tpu_custom_call" | custom-call | flops 1000 | bytes 1000 | tf_op jit(solution)/shard_map/pallas_call | solution.py:24
  3.7 2.1 %collective-permute-start.1 = (f32[104,1536]{1,0:T(8,128)S(1)}, f32[104,1536]{1,0:T(8,128)S(1)}, u32[]{:S(2)}, u32[]{:S(2)}) collective-permute-start(f32[104,1536]{1,0:T(8,128)S(1)} %get-tuple-element.23), channel_id=1, source_target_pairs={{1,0},{2,1},{3,2},{4,3},{5,4},{6,5},{7,6},{8,7},{9,8},{10,9},{11,1... | collective-permute-start | bytes 1916936 | tf_op jit(solution)/shard_map/ppermute | solution.py:505
  5.8 2.2 %collective-permute-start = (f32[104,1536]{1,0:T(8,128)S(1)}, f32[104,1536]{1,0:T(8,128)S(1)}, u32[]{:S(2)}, u32[]{:S(2)}) collective-permute-start(f32[104,1536]{1,0:T(8,128)S(1)} %get-tuple-element.32), channel_id=1, source_target_pairs={{0,1},{1,2},{2,3},{3,4},{4,5},{5,6},{6,7},{7,8},{8,9},{9,10},{10,1... | collective-permute-start | bytes 1916936 | tf_op jit(solution)/shard_map/ppermute | solution.py:504
  8.1 0.0 copy-done.2
  8.1 0.0 copy-done.3
  8.1 0.0 copy-done.1
  8.1 5.9 %shard_map.112 = (f32[1,128]{1,0:T(1,128)}, f32[4,48,1536]{2,1,0:T(8,128)}, f32[4,48,1536]{2,1,0:T(8,128)}, f32[8,128]{1,0:T(8,128)S(1)}, f32[4,12,80,128]{3,2,1...) custom-call(f32[4,48,1536]{2,1,0:T(8,128)} %bitcast.17, ...), custom_call_target="tpu_custom_call" | custom-call | flops 99999997952 | bytes 1000 | tf_op jit(solution)/shard_map/pallas_call | solution.py:24
  14.0 0.0 collective-permute-done.1.refs_7_
  14.0 3.5 %collective-permute-done.refs_6_ = f32[104,1536]{1,0:T(8,128)S(1)} collective-permute-done((f32[104,1536]{1,0:T(8,128)S(1)}, f32[104,1536]{1,0:T(8,128)S(1)}, u32[]{:S(2)}, u32[]{:S(2)}) %collective-permute-start) | collective-permute-done | bytes 639008 | tf_op jit(solution)/shard_map/ppermute | solution.py:504
  17.5 6.7 %shard_map.113 = (f32[4,48,1536]{2,1,0:T(8,128)S(1)}, f32[48,1536]{1,0:T(8,128)}, f32[104,1536]{1,0:T(8,128)}, f32[104,1536]{1,0:T(8,128)}, f32[4,12,80,128]{3,2...) custom-call(f32[4,12,80,128]{3,2,1,0:T(8,128)S(1)} %get-tuple-elemen, ...), custom_call_target="tpu_custom_call", output_to_operand_aliasing={{4}: (0, {}), {5}: (1, {}), {6}: (2, {}), {7}: (3, {}), {8}... | custom-call | flops 1000 | bytes 1000 | tf_op jit(solution)/shard_map/pallas_call | solution.py:24
  24.2 4.5 %collective-permute-start.2 = (f32[4,48,1536]{2,1,0:T(8,128)S(1)}, f32[4,48,1536]{2,1,0:T(8,128)S(1)}, u32[]{:S(2)}, u32[]{:S(2)}) collective-permute-start(f32[4,48,1536]{2,1,0:T(8,128)S(1)} %get-tuple-element.33.moved), channel_id=1, source_target_pairs={{0,32},{32,64},{64,96},{1,33},{33,65},{65,97},{2,34},{34,66},{66,9... | collective-permute-start | bytes 3538952 | tf_op jit(solution)/shard_map/ppermute | solution.py:511
  28.7 1.3 %collective-permute-start.4 = (f32[48,1536]{1,0:T(8,128)}, f32[48,1536]{1,0:T(8,128)}, u32[]{:S(2)}, u32[]{:S(2)}) collective-permute-start(f32[48,1536]{1,0:T(8,128)} %get-tuple-element.37), channel_id=1, source_target_pairs={{32,0},{64,32},{96,64},{33,1},{65,33},{97,65},{34,2},{66,34},{98,6... | collective-permute-start | bytes 884744 | tf_op jit(solution)/shard_map/ppermute | solution.py:512
  30.0 0.7 %collective-permute-done.3.incoming = f32[4,48,1536]{2,1,0:T(8,128)S(1)} collective-permute-done((f32[4,48,1536]{2,1,0:T(8,128)}, f32[4,48,1536]{2,1,0:T(8,128)S(1)}, u32[]{:S(2)}, u32[]{:S(2)}) %collective-permute-start.3) | collective-permute-done | bytes 1179680 | tf_op jit(solution)/shard_map/ppermute | solution.py:502
  30.8 0.2 shard_map.114
  31.0 0.0 copy-start
  31.0 0.6 copy-done
  31.7 13.3 %all-to-all-start = ((f32[128,1,128]{2,1,0:T(1,128)}), f32[128,1,128]{2,1,0:T(1,128)}, u32[]{:S(2)}, u32[]{:S(2)}) async-start(f32[128,1,128]{2,1,0:T(1,128)} %bitcast.11), calls=%async_computation | async-start | bytes 131072 | tf_op jit(solution)/shard_map/all_to_all | solution.py:514
  45.0 0.0 collective-permute-done.4.rims
  45.0 10.9 %shard_map.116 = f32[4,48,1536]{2,1,0:T(8,128)} custom-call(f32[4,48,1536]{2,1,0:T(8,128)S(1)} %collective-permute-done.3.incoming, f32[48,1536]{1,0:T(8,128)} %collective-permute-done.4.rims, f32[4,48,1536]{2,1,0:T(8,128)} %get-tuple-element.38.inc_base, bf16[2,4,48,1536]{3,2,1,0:T(8,128)(2,1)} %bitcast.14, s32[48,1536]{1,0:T(8,128)} %wake.5, ...), custom_call_target="tpu_custom_call" | custom-call | flops 1000 | bytes 1000 | tf_op jit(solution)/shard_map/pallas_call | solution.py:24
  55.9 4.2 %all-to-all-done = f32[128,1,128]{2,1,0:T(1,128)} async-done(((f32[128,1,128]{2,1,0:T(1,128)}), f32[128,1,128]{2,1,0:T(1,128)}, u32[]{:S(2)}, u32[]{:S(2)}) %all-to-all-start) | async-done | bytes 65568 | tf_op jit(solution)/shard_map/all_to_all | solution.py:514
  60.1 0.0 collective-permute-done.2.moved
  60.1 2.5 %shard_map.115 = (f32[4,48,1536]{2,1,0:T(8,128)}, f32[1,1]{1,0:T(1,128)}) custom-call(f32[4,48,1536]{2,1,0:T(8,128)} %get-tuple-element.25.base, f32[4,48,1536]{2,1,0:T(8,128)S(1)} %collective-permute-done.2.moved, f32[128,128]{1,0:T(8,128)} %bitcast.6.parts), custom_call_target="tpu_custom_call" | custom-call | flops 1000 | bytes 1000 | tf_op jit(solution)/shard_map/pallas_call | solution.py:24
Async XLA Ops:
  0.6 7.4 %copy-start.2 = (f32[1,128]{1,0:T(1,128)S(1)}, f32[1,128]{1,0:T(1,128)}, u32[]{:S(2)}) copy-start(f32[1,128]{1,0:T(1,128)} %obs_var.1) | copy-start | bytes 1540
  0.6 7.4 %copy-start.3 = (s32[1,128]{1,0:T(1,128)S(1)}, s32[1,128]{1,0:T(1,128)}, u32[]{:S(2)}) copy-start(s32[1,128]{1,0:T(1,128)} %cell.1) | copy-start | bytes 1540
  0.7 7.4 %copy-start.1 = (f32[1,128]{1,0:T(1,128)S(1)}, f32[1,128]{1,0:T(1,128)}, u32[]{:S(2)}) copy-start(f32[1,128]{1,0:T(1,128)} %dual.1) | copy-start | bytes 1540
  0.7 30.1 %collective-permute-start.3 = (f32[4,48,1536]{2,1,0:T(8,128)}, f32[4,48,1536]{2,1,0:T(8,128)S(1)}, u32[]{:S(2)}, u32[]{:S(2)}) collective-permute-start(f32[4,48,1536]{2,1,0:T(8,128)} %bitcast.18), channel_id=1, source_target_pairs={{32,0},{64,32},{96,64},{33,1},{65,33},{97,65},{34,2},{66,34},{98,6... | collective-permute-start | bytes 3538952 | tf_op jit(solution)/shard_map/ppermute | solution.py:502
  3.7 10.3 %collective-permute-start.1 = (f32[104,1536]{1,0:T(8,128)S(1)}, f32[104,1536]{1,0:T(8,128)S(1)}, u32[]{:S(2)}, u32[]{:S(2)}) collective-permute-start(f32[104,1536]{1,0:T(8,128)S(1)} %get-tuple-element.23), channel_id=1, source_target_pairs={{1,0},{2,1},{3,2},{4,3},{5,4},{6,5},{7,6},{8,7},{9,8},{10,9},{11,1... | collective-permute-start | bytes 1916936 | tf_op jit(solution)/shard_map/ppermute | solution.py:505
  5.8 11.7 %collective-permute-start = (f32[104,1536]{1,0:T(8,128)S(1)}, f32[104,1536]{1,0:T(8,128)S(1)}, u32[]{:S(2)}, u32[]{:S(2)}) collective-permute-start(f32[104,1536]{1,0:T(8,128)S(1)} %get-tuple-element.32), channel_id=1, source_target_pairs={{0,1},{1,2},{2,3},{3,4},{4,5},{5,6},{6,7},{7,8},{8,9},{9,10},{10,1... | collective-permute-start | bytes 1916936 | tf_op jit(solution)/shard_map/ppermute | solution.py:504
  24.2 35.9 %collective-permute-start.2 = (f32[4,48,1536]{2,1,0:T(8,128)S(1)}, f32[4,48,1536]{2,1,0:T(8,128)S(1)}, u32[]{:S(2)}, u32[]{:S(2)}) collective-permute-start(f32[4,48,1536]{2,1,0:T(8,128)S(1)} %get-tuple-element.33.moved), channel_id=1, source_target_pairs={{0,32},{32,64},{64,96},{1,33},{33,65},{65,97},{2,34},{34,66},{66,9... | collective-permute-start | bytes 3538952 | tf_op jit(solution)/shard_map/ppermute | solution.py:511
  28.7 16.2 %collective-permute-start.4 = (f32[48,1536]{1,0:T(8,128)}, f32[48,1536]{1,0:T(8,128)}, u32[]{:S(2)}, u32[]{:S(2)}) collective-permute-start(f32[48,1536]{1,0:T(8,128)} %get-tuple-element.37), channel_id=1, source_target_pairs={{32,0},{64,32},{96,64},{33,1},{65,33},{97,65},{34,2},{66,34},{98,6... | collective-permute-start | bytes 884744 | tf_op jit(solution)/shard_map/ppermute | solution.py:512
  31.0 0.6 copy-start
  31.7 28.4 %all-to-all-start = ((f32[128,1,128]{2,1,0:T(1,128)}), f32[128,1,128]{2,1,0:T(1,128)}, u32[]{:S(2)}, u32[]{:S(2)}) async-start(f32[128,1,128]{2,1,0:T(1,128)} %bitcast.11), calls=%async_computation | async-start | bytes 131072 | tf_op jit(solution)/shard_map/all_to_all | solution.py:514
